TPU v7x, 32 devices: a whole 2x2x4 slice. The times are simulated.
32 devices in a mesh: rep: 4 (over y, x), fsdp: 8 (over z, core).
Axes of the slice: x: 2, y: 2, z: 4, core: 2. Of those that a mesh axis runs over, the one named last changes fastest.
Arguments:
- tokens: bfloat16 [49152, 576], P(('rep', 'fsdp')), may hold values from -6 to 6
- segment: int32 [49152], P(('rep', 'fsdp')), may hold values from -1 to 767, as said below
- attn_gain: bfloat16 [2, 576], P(None, 'fsdp'), may hold values from 0.099609375 to 1.8984375
- w_query: bfloat16 [2, 576, 576], P(None, 'fsdp'), may hold values from -0.25 to 0.25
- key_weight: bfloat16 [2, 576, 192], P(None, 'fsdp'), may hold values from -0.25 to 0.25
- value_weight: bfloat16 [2, 576, 192], P(None, 'fsdp'), may hold values from -0.25 to 0.25
- w_out: bfloat16 [2, 576, 576], P(None, 'fsdp'), may hold values from -3 to 3
- mlp_gain: bfloat16 [2, 576], P(None, 'fsdp'), may hold values from 0.099609375 to 1.8984375
- gate_weight: bfloat16 [2, 576, 1536], P(None, 'fsdp'), may hold values from -0.25 to 0.25
- up_weight: bfloat16 [2, 576, 1536], P(None, 'fsdp'), may hold values from -0.25 to 0.25
- down_weight: bfloat16 [2, 1536, 576], P(None, 'fsdp'), may hold values from -0.15625 to 0.15625
- cotangent: bfloat16 [49152, 576], P(('rep', 'fsdp')), may hold values from -6 to 6
Outputs:
- out_tokens: bfloat16 [49152, 576], P(('rep', 'fsdp'))
- grad_tokens: float32 [49152, 576], P(('rep', 'fsdp'))
- grad_attn_gain: float32 [2, 576], P(None, 'fsdp')
- grad_query: float32 [2, 576, 576], P(None, 'fsdp')
- grad_key: float32 [2, 576, 192], P(None, 'fsdp')
- grad_value: float32 [2, 576, 192], P(None, 'fsdp')
- grad_out: float32 [2, 576, 576], P(None, 'fsdp')
- grad_mlp_gain: float32 [2, 576], P(None, 'fsdp')
- grad_gate: float32 [2, 576, 1536], P(None, 'fsdp')
- grad_up: float32 [2, 576, 1536], P(None, 'fsdp')
- grad_down: float32 [2, 1536, 576], P(None, 'fsdp')
Inputs may be any that keep to these rules, and one draw needn't show every extreme that they name: `segment`: each aligned block of 768 rows (one micro-batch of one device) holds whole sequences numbered 0, 1, 2, ... in order, then padding rows marked -1; no sequence has more than 512 rows and one has exactly 512; some block has no padding; some block holds 768 sequences of one row each.
All inputs are finite; a program needn't handle non-finite values.
Results may differ from a plain program's by a relative error of at most 0.025.
Values may be sent and summed in bfloat16 or wider, within the bound.
A program may use at most 384 MiB of HBM per device.

v0:
```python
import jax
import jax.numpy as jnp
from jax import lax
from jax.sharding import PartitionSpec as P

QUERY_HEADS = 9
KEY_VALUE_HEADS = 3
HEAD_WIDTH = 64
DECODER_LAYERS = 2
MICRO = 2


epsilon = 1e-05
rope_base = 100000.0
masked_fill = -1e30


def geometry(segment):
    count_of_rows = segment.shape[-1]
    row_index = jnp.arange(count_of_rows, dtype=jnp.int32)
    same_segment = segment[..., :, None] == segment[..., None, :]
    earlier = row_index[None, :] < row_index[:, None]
    position = jnp.sum(jnp.where(same_segment & earlier, 1, 0).astype(jnp.int32), axis=-1)
    allowed = same_segment & (row_index[None, :] <= row_index[:, None])
    active_rows = jnp.where(segment >= 0, 1.0, 0.0).astype(jnp.float32)[..., None]
    frequency = rope_base ** (-2.0 * jnp.arange(HEAD_WIDTH // 2, dtype=jnp.float32) / HEAD_WIDTH)
    angles = position.astype(jnp.float32)[..., None] * frequency
    return (allowed, active_rows, jnp.cos(angles)[..., None, :], jnp.sin(angles)[..., None, :])


def rotary_apply(vectors, cosine_table, sine_values):
    half_width = vectors.shape[-1] // 2
    first_half = vectors[..., :half_width]
    second_half = vectors[..., half_width:]
    return jnp.concatenate(
        [
            first_half * cosine_table - second_half * sine_values,
            second_half * cosine_table + first_half * sine_values,
        ],
        axis=-1,
    )


def rotary_inverse(vectors, cosine_table, sine_values):
    half_width = vectors.shape[-1] // 2
    first_half = vectors[..., :half_width]
    second_half = vectors[..., half_width:]
    return jnp.concatenate(
        [
            first_half * cosine_table + second_half * sine_values,
            second_half * cosine_table - first_half * sine_values,
        ],
        axis=-1,
    )


def norm_forward(value_rows, gain_row):
    factor = lax.rsqrt(jnp.mean(value_rows * value_rows, axis=-1, keepdims=True) + epsilon)
    return (value_rows * factor * gain_row, factor)


def norm_backward(value_rows, factor, gain_row, upstream):
    scaled = upstream * gain_row
    through = factor * scaled - value_rows * (factor * factor * factor) * jnp.mean(
        scaled * value_rows, axis=-1, keepdims=True
    )
    return (through, jnp.sum(upstream * value_rows * factor, axis=0))


def project_attention(residual, params, layout):
    allowed, active_rows, cosine_table, sine_values = layout
    count_of_rows = residual.shape[0]
    normed, factor = norm_forward(residual, params[0].astype(jnp.float32))
    normed = normed.astype(jnp.bfloat16)
    query_rows = jnp.dot(normed, params[1], preferred_element_type=jnp.float32).reshape(
        count_of_rows, QUERY_HEADS, HEAD_WIDTH
    )
    keys_raw = jnp.dot(normed, params[2], preferred_element_type=jnp.float32).reshape(
        count_of_rows, KEY_VALUE_HEADS, HEAD_WIDTH
    )
    value_rows = (
        jnp.dot(normed, params[3], preferred_element_type=jnp.float32)
        .astype(jnp.bfloat16)
        .reshape(count_of_rows, KEY_VALUE_HEADS, HEAD_WIDTH)
    )
    query_rows = (
        rotary_apply(query_rows, cosine_table, sine_values)
        .astype(jnp.bfloat16)
        .reshape(count_of_rows, KEY_VALUE_HEADS, QUERY_HEADS // KEY_VALUE_HEADS, HEAD_WIDTH)
    )
    key_rows = rotary_apply(keys_raw, cosine_table, sine_values).astype(jnp.bfloat16)
    scores = jnp.einsum(
        "qgjd,kgd->gjqk", query_rows, key_rows, preferred_element_type=jnp.float32
    ) * HEAD_WIDTH ** (-0.5)
    scores = jnp.where(allowed, scores, masked_fill)
    return (normed, factor, query_rows, key_rows, value_rows, scores)


def layer_forward(residual, params, layout):
    active_rows = layout[1]
    count_of_rows = residual.shape[0]
    normed, factor, query_rows, key_rows, value_rows, scores = project_attention(
        residual, params, layout
    )
    peak = jnp.max(scores, axis=-1, keepdims=True)
    expo = jnp.exp(scores - peak)
    total = jnp.sum(expo, axis=-1, keepdims=True)
    probs = (expo / total).astype(jnp.bfloat16)
    mixed = jnp.einsum("gjqk,kgd->qgjd", probs, value_rows, preferred_element_type=jnp.float32)
    mixed = mixed.reshape(count_of_rows, QUERY_HEADS * HEAD_WIDTH).astype(jnp.bfloat16)
    hidden_state = (
        residual + jnp.dot(mixed, params[4], preferred_element_type=jnp.float32) * active_rows
    )
    normed_feed_input, factor_mlp = norm_forward(hidden_state, params[5].astype(jnp.float32))
    normed_feed_input = normed_feed_input.astype(jnp.bfloat16)
    gate_branch = jnp.dot(normed_feed_input, params[6], preferred_element_type=jnp.float32)
    up_branch = jnp.dot(normed_feed_input, params[7], preferred_element_type=jnp.float32)
    inner_product = (jax.nn.silu(gate_branch) * up_branch).astype(jnp.bfloat16)
    output = (
        hidden_state
        + jnp.dot(inner_product, params[8], preferred_element_type=jnp.float32) * active_rows
    )
    return (output, peak + jnp.log(total))


def layer_backward(residual, log_total, params, layout, upstream):
    allowed, active_rows, cosine_table, sine_values = layout
    count_of_rows = residual.shape[0]
    scale = HEAD_WIDTH ** (-0.5)
    attn_gain_f = params[0].astype(jnp.float32)
    mlp_gain_f = params[5].astype(jnp.float32)
    normed, factor, query_rows, key_rows, value_rows, scores = project_attention(
        residual, params, layout
    )
    probs_full = jnp.exp(scores - log_total)
    probs = probs_full.astype(jnp.bfloat16)
    mixed = jnp.einsum("gjqk,kgd->qgjd", probs, value_rows, preferred_element_type=jnp.float32)
    mixed = mixed.reshape(count_of_rows, QUERY_HEADS * HEAD_WIDTH).astype(jnp.bfloat16)
    hidden_state = (
        residual + jnp.dot(mixed, params[4], preferred_element_type=jnp.float32) * active_rows
    )
    normed_feed_input, factor_mlp = norm_forward(hidden_state, mlp_gain_f)
    normed_feed_input = normed_feed_input.astype(jnp.bfloat16)
    gate_branch = jnp.dot(normed_feed_input, params[6], preferred_element_type=jnp.float32)
    up_branch = jnp.dot(normed_feed_input, params[7], preferred_element_type=jnp.float32)
    sigmoid_gate = jax.nn.sigmoid(gate_branch)
    activated = gate_branch * sigmoid_gate
    inner_product = (activated * up_branch).astype(jnp.bfloat16)
    grad_branch = (upstream * active_rows).astype(jnp.bfloat16)
    grad_down = jnp.einsum(
        "rf,rd->fd", inner_product, grad_branch, preferred_element_type=jnp.float32
    )
    grad_inner = jnp.einsum(
        "rd,fd->rf", grad_branch, params[8], preferred_element_type=jnp.float32
    ).astype(jnp.bfloat16)
    grad_gate_in = (
        grad_inner * up_branch * sigmoid_gate * (1.0 + gate_branch * (1.0 - sigmoid_gate))
    ).astype(jnp.bfloat16)
    grad_up_in = (grad_inner * activated).astype(jnp.bfloat16)
    grad_gate = jnp.einsum(
        "rd,rf->df", normed_feed_input, grad_gate_in, preferred_element_type=jnp.float32
    )
    grad_up = jnp.einsum(
        "rd,rf->df", normed_feed_input, grad_up_in, preferred_element_type=jnp.float32
    )
    grad_normed_mlp = jnp.einsum(
        "rf,df->rd", grad_gate_in, params[6], preferred_element_type=jnp.float32
    )
    grad_normed_mlp = grad_normed_mlp + jnp.einsum(
        "rf,df->rd", grad_up_in, params[7], preferred_element_type=jnp.float32
    )
    grad_hidden, grad_mlp_gain = norm_backward(
        hidden_state, factor_mlp, mlp_gain_f, grad_normed_mlp
    )
    grad_hidden = grad_hidden + upstream
    grad_attn = (grad_hidden * active_rows).astype(jnp.bfloat16)
    grad_out = jnp.einsum("re,rd->ed", mixed, grad_attn, preferred_element_type=jnp.float32)
    mixed_gradient = jnp.einsum(
        "rd,ed->re", grad_attn, params[4], preferred_element_type=jnp.float32
    ).astype(jnp.bfloat16)
    mixed_gradient = mixed_gradient.reshape(
        count_of_rows, KEY_VALUE_HEADS, QUERY_HEADS // KEY_VALUE_HEADS, HEAD_WIDTH
    )
    value_gradient = jnp.einsum(
        "gjqk,qgjd->kgd", probs, mixed_gradient, preferred_element_type=jnp.float32
    )
    value_gradient = value_gradient.reshape(count_of_rows, KEY_VALUE_HEADS * HEAD_WIDTH).astype(
        jnp.bfloat16
    )
    grad_probs = jnp.einsum(
        "qgjd,kgd->gjqk", mixed_gradient, value_rows, preferred_element_type=jnp.float32
    )
    row_weight = jnp.sum(probs_full * grad_probs, axis=-1, keepdims=True)
    grad_scores = (probs_full * (grad_probs - row_weight)).astype(jnp.bfloat16)
    grad_queries = (
        jnp.einsum("gjqk,kgd->qgjd", grad_scores, key_rows, preferred_element_type=jnp.float32)
        * scale
    )
    grad_queries = rotary_inverse(
        grad_queries.reshape(count_of_rows, QUERY_HEADS, HEAD_WIDTH), cosine_table, sine_values
    )
    grad_queries = grad_queries.reshape(count_of_rows, QUERY_HEADS * HEAD_WIDTH).astype(
        jnp.bfloat16
    )
    key_gradient = (
        jnp.einsum("gjqk,qgjd->kgd", grad_scores, query_rows, preferred_element_type=jnp.float32)
        * scale
    )
    key_gradient = (
        rotary_inverse(key_gradient, cosine_table, sine_values)
        .reshape(count_of_rows, KEY_VALUE_HEADS * HEAD_WIDTH)
        .astype(jnp.bfloat16)
    )
    grad_query = jnp.einsum("rd,re->de", normed, grad_queries, preferred_element_type=jnp.float32)
    grad_key = jnp.einsum("rd,re->de", normed, key_gradient, preferred_element_type=jnp.float32)
    grad_value = jnp.einsum("rd,re->de", normed, value_gradient, preferred_element_type=jnp.float32)
    grad_normed = jnp.einsum(
        "re,de->rd", grad_queries, params[1], preferred_element_type=jnp.float32
    )
    grad_normed = grad_normed + jnp.einsum(
        "re,de->rd", key_gradient, params[2], preferred_element_type=jnp.float32
    )
    grad_normed = grad_normed + jnp.einsum(
        "re,de->rd", value_gradient, params[3], preferred_element_type=jnp.float32
    )
    grad_input, grad_attn_gain = norm_backward(residual, factor, attn_gain_f, grad_normed)
    grad_terms = (
        grad_attn_gain,
        grad_query,
        grad_key,
        grad_value,
        grad_out,
        grad_mlp_gain,
        grad_gate,
        grad_up,
        grad_down,
    )
    return (grad_input + grad_hidden, grad_terms)


def fetch_forward_each(weight_list, layer_index):
    return (
        lax.all_gather(weight_list[0][layer_index], "fsdp", axis=0, tiled=True),
        lax.all_gather(weight_list[1][layer_index], "fsdp", axis=0, tiled=True),
        lax.all_gather(weight_list[2][layer_index], "fsdp", axis=0, tiled=True),
        lax.all_gather(weight_list[3][layer_index], "fsdp", axis=0, tiled=True),
        lax.all_gather(weight_list[4][layer_index], "fsdp", axis=0, tiled=True),
        lax.all_gather(weight_list[5][layer_index], "fsdp", axis=0, tiled=True),
        lax.all_gather(weight_list[6][layer_index], "fsdp", axis=0, tiled=True),
        lax.all_gather(weight_list[7][layer_index], "fsdp", axis=0, tiled=True),
        lax.all_gather(weight_list[8][layer_index], "fsdp", axis=0, tiled=True),
    )


def fetch_backward_each(weight_list, layer_index):
    return (
        lax.all_gather(weight_list[0][layer_index], "fsdp", axis=0, tiled=True),
        lax.all_gather(weight_list[1][layer_index], "fsdp", axis=0, tiled=True),
        lax.all_gather(weight_list[2][layer_index], "fsdp", axis=0, tiled=True),
        lax.all_gather(weight_list[3][layer_index], "fsdp", axis=0, tiled=True),
        lax.all_gather(weight_list[4][layer_index], "fsdp", axis=0, tiled=True),
        lax.all_gather(weight_list[5][layer_index], "fsdp", axis=0, tiled=True),
        lax.all_gather(weight_list[6][layer_index], "fsdp", axis=0, tiled=True),
        lax.all_gather(weight_list[7][layer_index], "fsdp", axis=0, tiled=True),
        lax.all_gather(weight_list[8][layer_index], "fsdp", axis=0, tiled=True),
    )


def local(
    tokens,
    segment,
    attn_gain,
    w_query,
    key_weight,
    value_weight,
    w_out,
    mlp_gain,
    gate_weight,
    up_weight,
    down_weight,
    cotangent,
):
    weight_list = [
        attn_gain,
        w_query,
        key_weight,
        value_weight,
        w_out,
        mlp_gain,
        gate_weight,
        up_weight,
        down_weight,
    ]
    batch_rows = tokens.shape[0] // MICRO
    residual = [
        tokens[batch_index * batch_rows : (batch_index + 1) * batch_rows].astype(jnp.float32)
        for batch_index in range(MICRO)
    ]
    layouts = [
        geometry(segment[batch_index * batch_rows : (batch_index + 1) * batch_rows])
        for batch_index in range(MICRO)
    ]
    saved_inputs = []
    saved_totals = []
    for layer_index in range(DECODER_LAYERS):
        layer_inputs = []
        layer_totals = []
        for batch_index in range(MICRO):
            current = fetch_forward_each(weight_list, layer_index)
            layer_inputs.append(residual[batch_index])
            residual[batch_index], log_total = layer_forward(
                residual[batch_index], current, layouts[batch_index]
            )
            layer_totals.append(log_total)
        saved_inputs.append(layer_inputs)
        saved_totals.append(layer_totals)
    out_tokens = jnp.concatenate(residual, axis=0).astype(jnp.bfloat16)
    upstream = [
        cotangent[batch_index * batch_rows : (batch_index + 1) * batch_rows].astype(jnp.float32)
        for batch_index in range(MICRO)
    ]
    layer_shards = [None] * DECODER_LAYERS
    for layer_index in reversed(range(DECODER_LAYERS)):
        summed = None
        for batch_index in reversed(range(MICRO)):
            current = fetch_backward_each(weight_list, layer_index)
            upstream[batch_index], grad_terms = layer_backward(
                saved_inputs[layer_index][batch_index],
                saved_totals[layer_index][batch_index],
                current,
                layouts[batch_index],
                upstream[batch_index],
            )
            if summed is None:
                summed = grad_terms
            else:
                summed = tuple(
                    (earlier_sum + new_term for earlier_sum, new_term in zip(summed, grad_terms))
                )
        shards = (
            lax.psum_scatter(
                summed[0].astype(jnp.bfloat16), "fsdp", scatter_dimension=0, tiled=True
            ).astype(jnp.float32),
            lax.psum_scatter(
                summed[1].astype(jnp.bfloat16), "fsdp", scatter_dimension=0, tiled=True
            ).astype(jnp.float32),
            lax.psum_scatter(
                summed[2].astype(jnp.bfloat16), "fsdp", scatter_dimension=0, tiled=True
            ).astype(jnp.float32),
            lax.psum_scatter(
                summed[3].astype(jnp.bfloat16), "fsdp", scatter_dimension=0, tiled=True
            ).astype(jnp.float32),
            lax.psum_scatter(
                summed[4].astype(jnp.bfloat16), "fsdp", scatter_dimension=0, tiled=True
            ).astype(jnp.float32),
            lax.psum_scatter(
                summed[5].astype(jnp.bfloat16), "fsdp", scatter_dimension=0, tiled=True
            ).astype(jnp.float32),
            lax.psum_scatter(
                summed[6].astype(jnp.bfloat16), "fsdp", scatter_dimension=0, tiled=True
            ).astype(jnp.float32),
            lax.psum_scatter(
                summed[7].astype(jnp.bfloat16), "fsdp", scatter_dimension=0, tiled=True
            ).astype(jnp.float32),
            lax.psum_scatter(
                summed[8].astype(jnp.bfloat16), "fsdp", scatter_dimension=0, tiled=True
            ).astype(jnp.float32),
        )
        shards = (
            lax.psum(shards[0].astype(jnp.bfloat16), "rep").astype(jnp.float32),
            lax.psum(shards[1].astype(jnp.bfloat16), "rep").astype(jnp.float32),
            lax.psum(shards[2].astype(jnp.bfloat16), "rep").astype(jnp.float32),
            lax.psum(shards[3].astype(jnp.bfloat16), "rep").astype(jnp.float32),
            lax.psum(shards[4].astype(jnp.bfloat16), "rep").astype(jnp.float32),
            lax.psum(shards[5].astype(jnp.bfloat16), "rep").astype(jnp.float32),
            lax.psum(shards[6].astype(jnp.bfloat16), "rep").astype(jnp.float32),
            lax.psum(shards[7].astype(jnp.bfloat16), "rep").astype(jnp.float32),
            lax.psum(shards[8].astype(jnp.bfloat16), "rep").astype(jnp.float32),
        )
        layer_shards[layer_index] = shards
    stacked = tuple(
        (
            jnp.stack([layer_shards[layer_index][member] for layer_index in range(DECODER_LAYERS)])
            for member in range(9)
        )
    )
    grad_tokens = jnp.concatenate(upstream, axis=0)
    return (
        out_tokens,
        grad_tokens,
        stacked[0],
        stacked[1],
        stacked[2],
        stacked[3],
        stacked[4],
        stacked[5],
        stacked[6],
        stacked[7],
        stacked[8],
    )


def solution(mesh):
    in_specs = (
        P(("rep", "fsdp"), None),
        P(("rep", "fsdp")),
        P(None, "fsdp"),
        P(None, "fsdp", None),
        P(None, "fsdp", None),
        P(None, "fsdp", None),
        P(None, "fsdp", None),
        P(None, "fsdp"),
        P(None, "fsdp", None),
        P(None, "fsdp", None),
        P(None, "fsdp", None),
        P(("rep", "fsdp"), None),
    )
    out_specs = (
        P(("rep", "fsdp"), None),
        P(("rep", "fsdp"), None),
        P(None, "fsdp"),
        P(None, "fsdp", None),
        P(None, "fsdp", None),
        P(None, "fsdp", None),
        P(None, "fsdp", None),
        P(None, "fsdp"),
        P(None, "fsdp", None),
        P(None, "fsdp", None),
        P(None, "fsdp", None),
    )
    return jax.shard_map(local, mesh=mesh, in_specs=in_specs, out_specs=out_specs, check_vma=False)
```

profile of v0, /device:TPU:0, one launch (start us, length us, event | category | flops | bytes accessed | tf_op | source)
XLA Modules:
  0.0 1177.9 jit_solution(14641799592724383515)
XLA Ops:
  16.1 19.0 %all-reduce.13 = (bf16[576]{0:T(1024)(128)(2,1)S(1)}, bf16[576]{0:T(1024)(128)(2,1)S(1)}, bf16[576]{0:T(1024)(128)(2,1)S(1)}, bf16[576]{0:T(1024)(128)(2,1)S(1)}) all-reduce(bf16[576]{0:T(1024)(128)(2,1)S(1)} %dynamic-update-slice, bf16[576]{0:T(1024)(128)(2,1)S(1)} %dynamic-update-slice.1, ...), channel_id=2, replica_groups=mesh['rep'=4,'fsdp'=8] {'fsdp'}, use_global_device_ids=true, to_apply=%add | all-reduce | flops 2304 | bytes 9216
  35.6 14.3 %all-gather.1 = bf16[1,576,192]{2,1,0:T(8,128)(2,1)S(1)} all-gather(bf16[1,72,192]{2,1,0:T(8,128)(2,1)S(1)} %get-tuple-element.114), channel_id=3, replica_groups=mesh['rep'=4,'fsdp'=8] {'fsdp'}, dimensions={1}, use_global_device_ids=true | all-gather | bytes 248832 | tf_op jit(solution)/shard_map/all_gather | solution.py:246
  49.8 15.3 %all-gather.2 = bf16[1,576,192]{2,1,0:T(8,128)(2,1)S(1)} all-gather(bf16[1,72,192]{2,1,0:T(8,128)(2,1)S(1)} %get-tuple-element.112), channel_id=4, replica_groups=mesh['rep'=4,'fsdp'=8] {'fsdp'}, dimensions={1}, use_global_device_ids=true | all-gather | bytes 248832 | tf_op jit(solution)/shard_map/all_gather | solution.py:245
  70.5 16.8 %all-gather.3 = bf16[1,576,576]{2,1,0:T(8,128)(2,1)S(1)} all-gather(bf16[1,72,576]{2,1,0:T(8,128)(2,1)S(1)} %get-tuple-element.110), channel_id=5, replica_groups=mesh['rep'=4,'fsdp'=8] {'fsdp'}, dimensions={1}, use_global_device_ids=true | all-gather | bytes 746496 | tf_op jit(solution)/shard_map/all_gather | solution.py:244
  90.7 16.3 %all-gather.10 = bf16[1,576,192]{2,1,0:T(8,128)(2,1)} all-gather(bf16[1,72,192]{2,1,0:T(8,128)(2,1)S(1)} %get-tuple-element.113), channel_id=12, replica_groups=mesh['rep'=4,'fsdp'=8] {'fsdp'}, dimensions={1}, use_global_device_ids=true | all-gather | bytes 248832 | tf_op jit(solution)/shard_map/all_gather | solution.py:246
  106.9 16.3 %all-gather.11 = bf16[1,576,192]{2,1,0:T(8,128)(2,1)} all-gather(bf16[1,72,192]{2,1,0:T(8,128)(2,1)S(1)} %get-tuple-element.111), channel_id=13, replica_groups=mesh['rep'=4,'fsdp'=8] {'fsdp'}, dimensions={1}, use_global_device_ids=true | all-gather | bytes 248832 | tf_op jit(solution)/shard_map/all_gather | solution.py:245
  123.2 18.7 %all-gather.13 = bf16[1,576,576]{2,1,0:T(8,128)(2,1)} all-gather(bf16[1,72,576]{2,1,0:T(8,128)(2,1)S(1)} %get-tuple-element.107), channel_id=15, replica_groups=mesh['rep'=4,'fsdp'=8] {'fsdp'}, dimensions={1}, use_global_device_ids=true | all-gather | bytes 746496 | tf_op jit(solution)/shard_map/all_gather | solution.py:247
  141.9 19.2 %all-gather.12 = bf16[1,576,576]{2,1,0:T(8,128)(2,1)} all-gather(bf16[1,72,576]{2,1,0:T(8,128)(2,1)S(1)} %get-tuple-element.109), channel_id=14, replica_groups=mesh['rep'=4,'fsdp'=8] {'fsdp'}, dimensions={1}, use_global_device_ids=true | all-gather | bytes 746496 | tf_op jit(solution)/shard_map/all_gather | solution.py:244
  161.1 17.7 %all-gather.4 = bf16[1,576,576]{2,1,0:T(8,128)(2,1)S(1)} all-gather(bf16[1,72,576]{2,1,0:T(8,128)(2,1)S(1)} %get-tuple-element.108), channel_id=6, replica_groups=mesh['rep'=4,'fsdp'=8] {'fsdp'}, dimensions={1}, use_global_device_ids=true | all-gather | bytes 746496 | tf_op jit(solution)/shard_map/all_gather | solution.py:247
  195.9 10.4 fusion.158
  220.8 13.9 %fusion.171 = bf16[3,64,3,768]{3,1,2,0:T(8,128)(2,1)} fusion(bf16[768,3,64,1]{0,2,3,1:T(8,128)(2,1)S(1)} %bitcast.661, f32[3,3,768,768]{2,3,1,0:T(8,128)S(1)} %get-tuple-element.157, f32[3,3,768]{2,1,0:T(4,128)S(1)} %fusion.14, f32[3,3,768]{2,1,0:T(4,128)} %copy-done.188), kind=kOutput, calls=%fused_computation.283 | convolution fusion | flops 695844864 | bytes 22468608 | tf_op jit(solution)/shard_map/gjqk,kgd->qgjd/dot_general | solution.py:109
  234.8 10.4 fusion.164
  314.2 10.5 fusion.167
  328.1 10.6 fusion.161
  396.6 13.4 %fusion.9 = (f32[3,3,768]{2,1,0:T(4,128)S(1)}, f32[3,768,768,3]{2,1,3,0:T(8,128)}) fusion(f32[3,3,768,768]{2,3,1,0:T(8,128)} %copy-done, f32[3,3,768]{2,1,0:T(4,128)S(1)} %copy-done.142, bf16[768,3,64,1]{0,2,3,1:T(8,128)(2,1)S(1)} %bitcast.628, bf16[768,3,3,64]{0,3,2,1:T(8,128)(2,1)S(1)} %bitcast.595), kind=kOutput, calls=%fused_computation.17 | convolution fusion | flops 695395584 | bytes 43702272 | tf_op jit(solution)/shard_map/qgjd,kgd->gjqk/dot_general | solution.py:190
  409.9 14.3 %fusion.11 = bf16[3,3,768,768]{2,3,1,0:T(8,128)(2,1)S(1)} fusion(f32[3,768,768,3]{2,1,3,0:T(8,128)} %get-tuple-element.185, f32[3,3,768,768]{2,3,1,0:T(8,128)} %copy-done, f32[3,3,768]{2,1,0:T(4,128)S(1)} %get-tuple-element.184, f32[3,3,768]{2,1,0:T(4,128)S(1)} %copy-done.142), kind=kLoop, calls=%fused_computation.19 | loop fusion | flops 21233664 | bytes 53139456 | tf_op jit(solution)/shard_map/convert_element_type | solution.py:194
  440.6 13.4 %fusion.3 = (f32[3,3,768]{2,1,0:T(4,128)S(1)}, f32[3,768,768,3]{2,1,3,0:T(8,128)}) fusion(f32[3,3,768,768]{2,3,1,0:T(8,128)} %copy-done.1, f32[3,3,768]{2,1,0:T(4,128)S(1)} %copy-done.140, bf16[768,3,64,1]{0,2,3,1:T(8,128)(2,1)S(1)} %bitcast.625, bf16[768,3,3,64]{0,3,2,1:T(8,128)(2,1)S(1)} %bitcast.597), kind=kOutput, calls=%fused_computation.7 | convolution fusion | flops 695395584 | bytes 43702272 | tf_op jit(solution)/shard_map/qgjd,kgd->gjqk/dot_general | solution.py:190
  454.0 14.7 %fusion.5 = bf16[3,3,768,768]{2,3,1,0:T(8,128)(2,1)S(1)} fusion(f32[3,768,768,3]{2,1,3,0:T(8,128)} %get-tuple-element.187, f32[3,3,768,768]{2,3,1,0:T(8,128)} %copy-done.1, f32[3,3,768]{2,1,0:T(4,128)S(1)} %get-tuple-element.186, f32[3,3,768]{2,1,0:T(4,128)S(1)} %copy-done.140), kind=kLoop, calls=%fused_computation.9 | loop fusion | flops 21233664 | bytes 53139456 | tf_op jit(solution)/shard_map/convert_element_type | solution.py:194
  530.6 13.9 %fusion = (f32[3,3,768]{2,1,0:T(4,128)}, f32[3,768,768,3]{2,1,3,0:T(8,128)}) fusion(f32[3,3,768,768]{2,3,1,0:T(8,128)} %copy-done.3, f32[3,3,768]{2,1,0:T(4,128)S(1)} %copy-done.138, bf16[768,3,64,1]{0,2,3,1:T(8,128)(2,1)S(1)} %bitcast.663, bf16[768,3,3,64]{0,3,2,1:T(8,128)(2,1)S(1)} %bitcast.593), kind=kOutput, calls=%fused_computation.2 | convolution fusion | flops 695395584 | bytes 43702272 | tf_op jit(solution)/shard_map/qgjd,kgd->gjqk/dot_general | solution.py:190
  554.9 14.1 %fusion.6 = (f32[3,3,768]{2,1,0:T(4,128)}, f32[3,768,768,3]{2,1,3,0:T(8,128)}) fusion(f32[3,3,768,768]{2,3,1,0:T(8,128)} %copy-done.2, f32[3,3,768]{2,1,0:T(4,128)S(1)} %copy-done.135, bf16[768,3,64,1]{0,2,3,1:T(8,128)(2,1)S(1)} %bitcast.660, bf16[768,3,3,64]{0,3,2,1:T(8,128)(2,1)S(1)} %bitcast.591), kind=kOutput, calls=%fused_computation.12 | convolution fusion | flops 695395584 | bytes 43702272 | tf_op jit(solution)/shard_map/qgjd,kgd->gjqk/dot_general | solution.py:190
  572.7 14.7 %fusion.2 = bf16[3,3,768,768]{2,3,1,0:T(8,128)(2,1)S(1)} fusion(f32[3,768,768,3]{2,1,3,0:T(8,128)} %get-tuple-element.200, f32[3,3,768,768]{2,3,1,0:T(8,128)} %copy-done.3, f32[3,3,768]{2,1,0:T(4,128)} %get-tuple-element.199, f32[3,3,768]{2,1,0:T(4,128)} %copy-done.137), kind=kLoop, calls=%fused_computation.4 | loop fusion | flops 21233664 | bytes 53139456 | tf_op jit(solution)/shard_map/convert_element_type | solution.py:194
  591.5 14.4 %fusion.8 = bf16[3,3,768,768]{2,3,1,0:T(8,128)(2,1)S(1)} fusion(f32[3,768,768,3]{2,1,3,0:T(8,128)} %get-tuple-element.196, f32[3,3,768,768]{2,3,1,0:T(8,128)} %copy-done.2, f32[3,3,768]{2,1,0:T(4,128)S(1)} %copy-done.179, f32[3,3,768]{2,1,0:T(4,128)S(1)} %copy-done.136), kind=kLoop, calls=%fused_computation.14 | loop fusion | flops 21233664 | bytes 53139456 | tf_op jit(solution)/shard_map/convert_element_type | solution.py:194
  700.2 15.5 %all-reduce.12 = (bf16[576]{0:T(1024)(128)(2,1)S(1)}, bf16[576]{0:T(1024)(128)(2,1)S(1)}, bf16[576]{0:T(1024)(128)(2,1)S(1)}, bf16[576]{0:T(1024)(128)(2,1)S(1)}) all-reduce(bf16[576]{0:T(1024)(128)(2,1)} %add_convert_fusion.30, bf16[576]{0:T(1024)(128)(2,1)S(1)} %add_convert_fusion.31, ...), channel_id=21, replica_groups=mesh['rep'=4,'fsdp'=8] {'fsdp'}, use_global_device_ids=true, to_apply=%region_40.41.clone | all-reduce | flops 2304 | bytes 9216
  799.2 32.2 %reduce-scatter.43.cloned.1.call-done = bf16[72,576]{1,0:T(8,128)(2,1)} async-done(((bf16[576,576]{1,0:T(8,128)(2,1)}), bf16[72,576]{1,0:T(8,128)(2,1)}) %reduce-scatter.43.cloned.1.call-update) | async-done | bytes 82960
  831.4 36.0 %reduce-scatter.41.cloned.1.call-done = bf16[192,576]{1,0:T(8,128)(2,1)} async-done(((bf16[1536,576]{1,0:T(8,128)(2,1)}), bf16[192,576]{1,0:T(8,128)(2,1)}) %reduce-scatter.41.cloned.1.call-update) | async-done | bytes 221200 | tf_op jit(solution)/shard_map/reduce_scatter | solution.py:365
  867.4 35.5 %reduce-scatter.33.cloned.1.call-done = bf16[72,1536]{1,0:T(8,128)(2,1)} async-done(((bf16[576,1536]{1,0:T(8,128)(2,1)}), bf16[72,1536]{1,0:T(8,128)(2,1)}) %reduce-scatter.33.cloned.1.call-update) | async-done | bytes 221200 | tf_op jit(solution)/shard_map/reduce_scatter | solution.py:359
  903.0 35.4 %reduce-scatter.37.cloned.1.call-done = bf16[72,1536]{1,0:T(8,128)(2,1)} async-done(((bf16[576,1536]{1,0:T(8,128)(2,1)}), bf16[72,1536]{1,0:T(8,128)(2,1)}) %reduce-scatter.37.cloned.1.call-update) | async-done | bytes 221200 | tf_op jit(solution)/shard_map/reduce_scatter | solution.py:362
  938.3 36.7 %reduce-scatter.39.cloned.1.call-done = bf16[192,576]{1,0:T(8,128)(2,1)} async-done(((bf16[1536,576]{1,0:T(8,128)(2,1)}), bf16[192,576]{1,0:T(8,128)(2,1)}) %reduce-scatter.39.cloned.1.call-update) | async-done | bytes 221200 | tf_op jit(solution)/shard_map/reduce_scatter | solution.py:365
  975.0 35.6 %reduce-scatter.31.cloned.1.call-done = bf16[72,1536]{1,0:T(8,128)(2,1)} async-done(((bf16[576,1536]{1,0:T(8,128)(2,1)}), bf16[72,1536]{1,0:T(8,128)(2,1)}) %reduce-scatter.31.cloned.1.call-update) | async-done | bytes 221200 | tf_op jit(solution)/shard_map/reduce_scatter | solution.py:359
  1010.6 35.2 %reduce-scatter.35.cloned.1.call-done = bf16[72,1536]{1,0:T(8,128)(2,1)} async-done(((bf16[576,1536]{1,0:T(8,128)(2,1)}), bf16[72,1536]{1,0:T(8,128)(2,1)}) %reduce-scatter.35.cloned.1.call-update) | async-done | bytes 221200 | tf_op jit(solution)/shard_map/reduce_scatter | solution.py:362
  1053.7 38.5 %all-reduce.19.cloned.1.call-done = (bf16[1,72]{1,0:T(2,128)(2,1)}, bf16[1,72]{1,0:T(2,128)(2,1)}, bf16[1,72,192]{2,1,0:T(8,128)(2,1)}, bf16[1,72,192]{2,1,0:T(8...) async-done(((bf16[1,72]{1,0:T(2,128)(2,1)}, bf16[1,72]{1,0:T(2,128)(2,1)}, ...) | async-done | bytes 111184 | tf_op jit(solution)/shard_map/psum | solution.py:370
  1097.6 65.7 %all-reduce.21.cloned.1.call-done = (bf16[1,72,576]{2,1,0:T(8,128)(2,1)}, bf16[1,72,576]{2,1,0:T(8,128)(2,1)}, bf16[1,72,576]{2,1,0:T(8,128)(2,1)}, bf16[1,72,57...) async-done(((bf16[1,72,576]{2,1,0:T(8,128)(2,1)}, ...) | async-done | bytes 1658896 | tf_op jit(solution)/shard_map/psum | solution.py:371
  (789 shorter events, 470.4 us)
Async XLA Ops:
  7.2 244.3 %all-gather.25.cloned.1.call-start = ((), (), s32[]{:S(2)}) async-start(), calls=%async_computation.24 | async-start | bytes 1990656 | tf_op jit(solution)/shard_map/all_gather | solution.py:249
  9.2 248.0 %all-gather.27.cloned.1.call-start = ((), (), s32[]{:S(2)}) async-start(), calls=%async_computation.25 | async-start | bytes 1990656 | tf_op jit(solution)/shard_map/all_gather | solution.py:250
  11.2 246.0 %all-gather.29.cloned.1.call-start = ((), (), s32[]{:S(2)}) async-start(), calls=%async_computation.26 | async-start | bytes 2211840 | tf_op jit(solution)/shard_map/all_gather | solution.py:251
  12.1 329.9 %all-gather.35.cloned.1.call-start = ((), (), s32[]{:S(2)}) async-start(), calls=%async_computation.29 | async-start | bytes 2211840 | tf_op jit(solution)/shard_map/all_gather | solution.py:251
  12.7 334.6 %all-gather.31.cloned.1.call-start = ((), (), s32[]{:S(2)}) async-start(), calls=%async_computation.27 | async-start | bytes 1990656 | tf_op jit(solution)/shard_map/all_gather | solution.py:249
  13.3 340.0 %all-gather.33.cloned.1.call-start = ((), (), s32[]{:S(2)}) async-start(), calls=%async_computation.28 | async-start | bytes 1990656 | tf_op jit(solution)/shard_map/all_gather | solution.py:250
  13.9 782.9 %reduce-scatter.29.cloned.1.call-start = ((), (), s32[]{:S(2)}) async-start(), calls=%async_computation.17 | async-start | bytes 331776 | tf_op jit(solution)/shard_map/reduce_scatter | solution.py:350
  66.4 168.4 %copy-start.132 = (bf16[768,192]{0,1:T(8,128)(2,1)}, bf16[768,192]{0,1:T(8,128)(2,1)S(1)}, u32[]{:S(2)}) copy-start(bf16[768,192]{0,1:T(8,128)(2,1)S(1)} %convolution_convert_fusion.9) | copy-start | bytes 884740
  66.9 128.9 %copy-start.130 = (bf16[768,192]{0,1:T(8,128)(2,1)}, bf16[768,192]{0,1:T(8,128)(2,1)S(1)}, u32[]{:S(2)}) copy-start(bf16[768,192]{0,1:T(8,128)(2,1)S(1)} %convolution_convert_fusion.11) | copy-start | bytes 884740
  70.5 110.6 %copy-start.154 = (pred[768,768]{0,1:T(8,128)(4,1)}, pred[768,768]{0,1:T(8,128)(4,1)S(1)}, u32[]{:S(2)}) copy-start(pred[768,768]{0,1:T(8,128)(4,1)S(1)} %get-tuple-element.205) | copy-start | bytes 1769476
  70.5 139.7 %copy-start.156 = (pred[768,768]{0,1:T(8,128)(4,1)}, pred[768,768]{0,1:T(8,128)(4,1)S(1)}, u32[]{:S(2)}) copy-start(pred[768,768]{0,1:T(8,128)(4,1)S(1)} %get-tuple-element.204) | copy-start | bytes 1769476
  89.4 183.4 %copy-start.194 = (f32[576]{0:T(1024)}, f32[576]{0:T(1024)S(1)}, u32[]{:S(2)}) copy-start(f32[576]{0:T(1024)S(1)} %convert_element_type.668) | copy-start | bytes 6916
  265.5 220.8 %copy-start.6 = (f32[768,576]{0,1:T(8,128)}, f32[768,576]{0,1:T(8,128)S(1)}, u32[]{:S(2)}) copy-start(f32[768,576]{0,1:T(8,128)S(1)} %get-tuple-element.165) | copy-start | bytes 5308420
  281.8 204.5 %copy-start.8 = (f32[768,576]{0,1:T(8,128)}, f32[768,576]{0,1:T(8,128)S(1)}, u32[]{:S(2)}) copy-start(f32[768,576]{0,1:T(8,128)S(1)} %get-tuple-element.167) | copy-start | bytes 5308420
  570.2 226.6 %reduce-scatter.25.cloned.1.call-start = ((), (), s32[]{:S(2)}) async-start(), calls=%async_computation.15 | async-start | bytes 331776 | tf_op jit(solution)/shard_map/reduce_scatter | solution.py:347
  611.4 185.4 %reduce-scatter.27.cloned.1.call-start = ((), (), s32[]{:S(2)}) async-start(), calls=%async_computation.16 | async-start | bytes 331776 | tf_op jit(solution)/shard_map/reduce_scatter | solution.py:350
  616.9 179.9 %reduce-scatter.23.cloned.1.call-start = ((), (), s32[]{:S(2)}) async-start(), calls=%async_computation.14 | async-start | bytes 331776 | tf_op jit(solution)/shard_map/reduce_scatter | solution.py:347
  620.4 176.6 %reduce-scatter.49.cloned.1.call-start = ((), (), s32[]{:S(2)}) async-start(), calls=%async_computation.33 | async-start | bytes 829440
  624.9 172.1 %reduce-scatter.45.cloned.1.call-start = ((), (), s32[]{:S(2)}) async-start(), calls=%async_computation.31 | async-start | bytes 829440
  632.2 167.0 %reduce-scatter.47.cloned.1.call-start = ((), (), s32[]{:S(2)}) async-start(), calls=%async_computation.32 | async-start | bytes 829440
  649.2 182.3 %reduce-scatter.43.cloned.1.call-start = ((), (), s32[]{:S(2)}) async-start(), calls=%async_computation.30 | async-start | bytes 829440
  656.0 211.4 %reduce-scatter.41.cloned.1.call-start = ((), (), s32[]{:S(2)}) async-start(), calls=%async_computation.23 | async-start | bytes 2211840 | tf_op jit(solution)/shard_map/reduce_scatter | solution.py:365
  670.3 232.6 %reduce-scatter.33.cloned.1.call-start = ((), (), s32[]{:S(2)}) async-start(), calls=%async_computation.19 | async-start | bytes 1990656 | tf_op jit(solution)/shard_map/reduce_scatter | solution.py:359
  677.6 260.7 %reduce-scatter.37.cloned.1.call-start = ((), (), s32[]{:S(2)}) async-start(), calls=%async_computation.21 | async-start | bytes 1990656 | tf_op jit(solution)/shard_map/reduce_scatter | solution.py:362
  692.4 282.6 %reduce-scatter.39.cloned.1.call-start = ((), (), s32[]{:S(2)}) async-start(), calls=%async_computation.22 | async-start | bytes 2211840 | tf_op jit(solution)/shard_map/reduce_scatter | solution.py:365
  733.1 277.5 %reduce-scatter.31.cloned.1.call-start = ((), (), s32[]{:S(2)}) async-start(), calls=%async_computation.18 | async-start | bytes 1990656 | tf_op jit(solution)/shard_map/reduce_scatter | solution.py:359
  750.7 295.1 %reduce-scatter.35.cloned.1.call-start = ((), (), s32[]{:S(2)}) async-start(), calls=%async_computation.20 | async-start | bytes 1990656 | tf_op jit(solution)/shard_map/reduce_scatter | solution.py:362
  768.3 323.9 %all-reduce.19.cloned.1.call-start = ((), (), s32[]{:S(2)}) async-start(), calls=%async_computation.34 | async-start | bytes 299008 | tf_op jit(solution)/shard_map/psum | solution.py:370
  787.4 261.4 %copy-start.31 = (f32[768,576]{0,1:T(8,128)S(1)}, f32[768,576]{0,1:T(8,128)}, u32[]{:S(2)}) copy-start(f32[768,576]{0,1:T(8,128)} %copy-done.30) | copy-start | bytes 5308420
  787.4 261.4 %copy-start.36 = (bf16[1536,576]{0,1:T(8,128)(2,1)S(1)}, bf16[1536,576]{0,1:T(8,128)(2,1)}, u32[]{:S(2)}) copy-start(bf16[1536,576]{0,1:T(8,128)(2,1)} %param.12) | copy-start | bytes 5308420
  796.8 249.1 %copy-start.222 = (f32[768]{0:T(1024)S(1)}, f32[768]{0:T(1024)}, u32[]{:S(2)}) copy-start(f32[768]{0:T(1024)} %get-tuple-element.27) | copy-start | bytes 9220
  796.8 366.5 %all-reduce.21.cloned.1.call-start = ((), (), s32[]{:S(2)}) async-start(), calls=%async_computation.35 | async-start | bytes 3489792 | tf_op jit(solution)/shard_map/psum | solution.py:371
  (246 other events, 1820.1 us)
Sparse Core Ops, SparseCore 0:
  10.2 30.3 all-gather.24
  42.8 28.0 all-gather.26
  73.1 29.7 all-gather.28
  104.4 33.9 all-gather.34
  139.8 31.7 all-gather.30
  173.1 25.2 all-gather.32
  570.3 29.2 reduce-scatter.28
  611.5 29.1 reduce-scatter.24
  643.0 28.6 reduce-scatter.26
  673.9 28.6 reduce-scatter.22
  704.9 29.8 reduce-scatter.48
  737.1 29.9 reduce-scatter.44
  769.3 29.8 reduce-scatter.46
  801.5 29.9 reduce-scatter.42
  833.6 33.7 reduce-scatter.40
  869.7 33.2 reduce-scatter.32
  905.2 33.0 reduce-scatter.36
  941.2 33.7 reduce-scatter.38
  977.3 33.2 reduce-scatter.30
  1012.7 33.0 reduce-scatter.34
  1050.0 42.1 all-reduce.18
  1097.2 66.1 all-reduce.20
where the time goes:
time: 1190 us; the launch traced here: 1180 us
  matrix products  467 us (39%)
  waiting for transfers between devices  355 us (30%)
  blocking collectives  169 us (14%)
  other arithmetic  119 us (10%)
  local copies, waits for them, and re-layouts  46.8 us (4%)
  between operations  19.1 us (2%)
    reduce_scatter x2, waiting for transfers between devices, local(): lax.psum_scatter(summed[8].astype(jnp.bfloat16), 'fsdp', scatter_dimensio...  72.6 us
    reduce_scatter x2, waiting for transfers between devices, local(): lax.psum_scatter(summed[6].astype(jnp.bfloat16), 'fsdp', scatter_dimensio...  71.2 us
    reduce_scatter x2, waiting for transfers between devices, local(): lax.psum_scatter(summed[7].astype(jnp.bfloat16), 'fsdp', scatter_dimensio...  70.6 us
    psum x1, waiting for transfers between devices, local(): lax.psum(shards[1].astype(jnp.bfloat16), 'rep').astype(jnp.float32)  65.7 us
    convert_element_type x4, other arithmetic, layer_backward(): grad_scores = (probs_full * (grad_probs - row_weight)).astype(jnp.bfloat16)  58.2 us
    dot_general x4, matrix products, layer_backward(): jnp.einsum('qgjd,kgd->gjqk', mixed_gradient, value_rows, preferred_elemen...  54.7 us
    dot_general x4, matrix products, layer_backward(): jnp.einsum('gjqk,kgd->qgjd', probs, value_rows, preferred_element_type=jn...  41.9 us
    unnamed x523, local copies, waits for them, and re-layouts  39.7 us
  transfers between devices with their start and end apart: 22, of which 10 were waited for; matrix products, arithmetic and copies ran while one was open for 32% of the time, Pallas kernels for 0%

commit v1 on v0

v1 whole, which is shorter than its diff:
```python
import jax
import jax.numpy as jnp
from jax import lax
from jax.sharding import PartitionSpec as P

QUERY_HEADS = 9
KEY_VALUE_HEADS = 3
HEAD_WIDTH = 64
DECODER_LAYERS = 2
MICRO = 2


epsilon = 1e-05
rope_base = 100000.0
masked_fill = -1e30


def geometry(segment):
    count_of_rows = segment.shape[-1]
    row_index = jnp.arange(count_of_rows, dtype=jnp.int32)
    same_segment = segment[..., :, None] == segment[..., None, :]
    earlier = row_index[None, :] < row_index[:, None]
    position = jnp.sum(jnp.where(same_segment & earlier, 1, 0).astype(jnp.int32), axis=-1)
    allowed = same_segment & (row_index[None, :] <= row_index[:, None])
    active_rows = jnp.where(segment >= 0, 1.0, 0.0).astype(jnp.float32)[..., None]
    frequency = rope_base ** (-2.0 * jnp.arange(HEAD_WIDTH // 2, dtype=jnp.float32) / HEAD_WIDTH)
    angles = position.astype(jnp.float32)[..., None] * frequency
    return (allowed, active_rows, jnp.cos(angles)[..., None, :], jnp.sin(angles)[..., None, :])


def rotary_apply(vectors, cosine_table, sine_values):
    half_width = vectors.shape[-1] // 2
    first_half = vectors[..., :half_width]
    second_half = vectors[..., half_width:]
    return jnp.concatenate(
        [
            first_half * cosine_table - second_half * sine_values,
            second_half * cosine_table + first_half * sine_values,
        ],
        axis=-1,
    )


def rotary_inverse(vectors, cosine_table, sine_values):
    half_width = vectors.shape[-1] // 2
    first_half = vectors[..., :half_width]
    second_half = vectors[..., half_width:]
    return jnp.concatenate(
        [
            first_half * cosine_table + second_half * sine_values,
            second_half * cosine_table - first_half * sine_values,
        ],
        axis=-1,
    )


def norm_forward(value_rows, gain_row):
    factor = lax.rsqrt(jnp.mean(value_rows * value_rows, axis=-1, keepdims=True) + epsilon)
    return (value_rows * factor * gain_row, factor)


def norm_backward(value_rows, factor, gain_row, upstream):
    scaled = upstream * gain_row
    through = factor * scaled - value_rows * (factor * factor * factor) * jnp.mean(
        scaled * value_rows, axis=-1, keepdims=True
    )
    return (through, jnp.sum(upstream * value_rows * factor, axis=0))


def attention_forward(query_rows, key_rows, value_rows, allowed):
    count_of_rows = query_rows.shape[0]
    queries = query_rows.reshape(
        count_of_rows, KEY_VALUE_HEADS, QUERY_HEADS // KEY_VALUE_HEADS, HEAD_WIDTH
    )
    keys = key_rows.reshape(count_of_rows, KEY_VALUE_HEADS, HEAD_WIDTH)
    values = value_rows.reshape(count_of_rows, KEY_VALUE_HEADS, HEAD_WIDTH)
    scores = jnp.einsum(
        "qgjd,kgd->gjqk", queries, keys, preferred_element_type=jnp.float32
    ) * HEAD_WIDTH ** (-0.5)
    scores = jnp.where(allowed, scores, masked_fill)
    peak = jnp.max(scores, axis=-1, keepdims=True)
    expo = jnp.exp(scores - peak)
    total = jnp.sum(expo, axis=-1, keepdims=True)
    probs = (expo / total).astype(jnp.bfloat16)
    mixed = jnp.einsum("gjqk,kgd->qgjd", probs, values, preferred_element_type=jnp.float32)
    mixed = mixed.reshape(count_of_rows, QUERY_HEADS * HEAD_WIDTH).astype(jnp.bfloat16)
    return (mixed, peak + jnp.log(total))


def attention_backward(query_rows, key_rows, value_rows, log_total, mixed_gradient, allowed):
    count_of_rows = query_rows.shape[0]
    scale = HEAD_WIDTH ** (-0.5)
    group_shape = (count_of_rows, KEY_VALUE_HEADS, QUERY_HEADS // KEY_VALUE_HEADS, HEAD_WIDTH)
    queries = query_rows.reshape(group_shape)
    keys = key_rows.reshape(count_of_rows, KEY_VALUE_HEADS, HEAD_WIDTH)
    values = value_rows.reshape(count_of_rows, KEY_VALUE_HEADS, HEAD_WIDTH)
    mixed_gradient = mixed_gradient.reshape(group_shape)
    scores = jnp.einsum("qgjd,kgd->gjqk", queries, keys, preferred_element_type=jnp.float32) * scale
    scores = jnp.where(allowed, scores, masked_fill)
    probs_full = jnp.exp(scores - log_total)
    probs = probs_full.astype(jnp.bfloat16)
    value_gradient = jnp.einsum(
        "gjqk,qgjd->kgd", probs, mixed_gradient, preferred_element_type=jnp.float32
    )
    grad_probs = jnp.einsum(
        "qgjd,kgd->gjqk", mixed_gradient, values, preferred_element_type=jnp.float32
    )
    row_weight = jnp.sum(probs_full * grad_probs, axis=-1, keepdims=True)
    grad_scores = (probs_full * (grad_probs - row_weight)).astype(jnp.bfloat16)
    grad_queries = (
        jnp.einsum("gjqk,kgd->qgjd", grad_scores, keys, preferred_element_type=jnp.float32) * scale
    )
    key_gradient = (
        jnp.einsum("gjqk,qgjd->kgd", grad_scores, queries, preferred_element_type=jnp.float32)
        * scale
    )
    return (
        grad_queries.reshape(count_of_rows, -1),
        key_gradient.reshape(count_of_rows, -1),
        value_gradient.reshape(count_of_rows, -1),
    )


def rotate_flat(rotation, rows, cosine_table, sine_values):
    shaped = rows.reshape(rows.shape[0], -1, HEAD_WIDTH)
    return rotation(shaped, cosine_table, sine_values).reshape(rows.shape).astype(jnp.bfloat16)


def layer_forward(residual, attn_params, fetch_feed, gains, layout):
    allowed, active_rows, cosine_table, sine_values = layout
    w_query, key_weight, value_weight, w_out = attn_params
    normed, factor = norm_forward(residual, gains[0])
    normed = normed.astype(jnp.bfloat16)
    query_rows = jnp.dot(normed, w_query, preferred_element_type=jnp.float32)
    key_rows = jnp.dot(normed, key_weight, preferred_element_type=jnp.float32)
    value_rows = jnp.dot(normed, value_weight, preferred_element_type=jnp.float32).astype(
        jnp.bfloat16
    )
    query_rows = rotate_flat(rotary_apply, query_rows, cosine_table, sine_values)
    key_rows = rotate_flat(rotary_apply, key_rows, cosine_table, sine_values)
    mixed, log_total = attend(query_rows, key_rows, value_rows, allowed)
    hidden_state = (
        residual + jnp.dot(mixed, w_out, preferred_element_type=jnp.float32) * active_rows
    )
    gate_weight, up_weight, down_weight = fetch_feed
    normed_feed, factor_mlp = norm_forward(hidden_state, gains[1])
    normed_feed = normed_feed.astype(jnp.bfloat16)
    gate_branch = jnp.dot(normed_feed, gate_weight, preferred_element_type=jnp.float32)
    up_branch = jnp.dot(normed_feed, up_weight, preferred_element_type=jnp.float32)
    inner_product = (jax.nn.silu(gate_branch) * up_branch).astype(jnp.bfloat16)
    output = (
        hidden_state
        + jnp.dot(inner_product, down_weight, preferred_element_type=jnp.float32) * active_rows
    )
    saved = (
        residual,
        normed,
        factor,
        query_rows,
        key_rows,
        value_rows,
        mixed,
        log_total,
        hidden_state,
        normed_feed,
        factor_mlp,
        gate_branch,
        up_branch,
        inner_product,
    )
    return (output, saved)


def contract_rows(left, right):
    return lax.dot_general(
        left, right, (((0,), (0,)), ((), ())), preferred_element_type=jnp.float32
    ).astype(jnp.bfloat16)


def times_transposed(left, right):
    return lax.dot_general(
        left, right, (((1,), (1,)), ((), ())), preferred_element_type=jnp.float32
    )


def feed_backward(saved, feed_params, gain_row, active_rows, upstream):
    hidden_state, normed_feed, factor_mlp, gate_branch, up_branch, inner_product = saved[8:]
    gate_weight, up_weight, down_weight = feed_params
    sigmoid_gate = jax.nn.sigmoid(gate_branch)
    activated = gate_branch * sigmoid_gate
    grad_branch = (upstream * active_rows).astype(jnp.bfloat16)
    grad_inner = times_transposed(grad_branch, down_weight).astype(jnp.bfloat16)
    grad_gate_in = (
        grad_inner * up_branch * sigmoid_gate * (1.0 + gate_branch * (1.0 - sigmoid_gate))
    ).astype(jnp.bfloat16)
    grad_up_in = (grad_inner * activated).astype(jnp.bfloat16)
    grad_down = contract_rows(inner_product, grad_branch)
    grad_gate = contract_rows(normed_feed, grad_gate_in)
    grad_up = contract_rows(normed_feed, grad_up_in)
    grad_normed = times_transposed(grad_gate_in, gate_weight) + times_transposed(
        grad_up_in, up_weight
    )
    through, grad_gain = norm_backward(hidden_state, factor_mlp, gain_row, grad_normed)
    return (through + upstream, grad_gain, (grad_gate, grad_up, grad_down))


def attention_part_backward(saved, attn_params, gain_row, layout, grad_hidden):
    residual, normed, factor, query_rows, key_rows, value_rows, mixed, log_total = saved[:8]
    w_query, key_weight, value_weight, w_out = attn_params
    allowed, active_rows, cosine_table, sine_values = layout
    grad_attn = (grad_hidden * active_rows).astype(jnp.bfloat16)
    grad_out = contract_rows(mixed, grad_attn)
    mixed_gradient = times_transposed(grad_attn, w_out).astype(jnp.bfloat16)
    grad_queries, key_gradient, value_gradient = attend_back(
        query_rows, key_rows, value_rows, log_total, mixed_gradient, allowed
    )
    value_gradient = value_gradient.astype(jnp.bfloat16)
    grad_queries = rotate_flat(rotary_inverse, grad_queries, cosine_table, sine_values)
    key_gradient = rotate_flat(rotary_inverse, key_gradient, cosine_table, sine_values)
    grad_query = contract_rows(normed, grad_queries)
    grad_key = contract_rows(normed, key_gradient)
    grad_value = contract_rows(normed, value_gradient)
    grad_normed = (
        times_transposed(grad_queries, w_query)
        + times_transposed(key_gradient, key_weight)
        + times_transposed(value_gradient, value_weight)
    )
    through, grad_gain = norm_backward(residual, factor, gain_row, grad_normed)
    return (through + grad_hidden, grad_gain, (grad_query, grad_key, grad_value, grad_out))


def blocks_of(rows):
    size = rows.shape[0] // MICRO
    return [rows[index * size : (index + 1) * size] for index in range(MICRO)]


def attend(query_rows, key_rows, value_rows, allowed):
    results = [
        attention_forward(*piece)
        for piece in zip(blocks_of(query_rows), blocks_of(key_rows), blocks_of(value_rows), allowed)
    ]
    return (jnp.concatenate([item[0] for item in results]), [item[1] for item in results])


def attend_back(query_rows, key_rows, value_rows, log_total, mixed_gradient, allowed):
    results = [
        attention_backward(*piece)
        for piece in zip(
            blocks_of(query_rows),
            blocks_of(key_rows),
            blocks_of(value_rows),
            log_total,
            blocks_of(mixed_gradient),
            allowed,
        )
    ]
    return tuple(jnp.concatenate([item[member] for item in results]) for member in range(3))


def sum_shards(buffer, last):
    shard = lax.psum_scatter(buffer, "fsdp", scatter_dimension=0, tiled=False)
    if last:
        return lax.psum(shard, "rep")
    rows, width = shard.shape
    copies = lax.axis_size("rep")
    padded = -(-rows // copies) * copies
    if padded != rows:
        shard = jnp.pad(shard, ((0, padded - rows), (0, 0)))
    part = lax.psum_scatter(shard, "rep", scatter_dimension=0, tiled=True)
    return lax.all_gather(part, "rep", axis=0, tiled=True)


def local(
    tokens,
    segment,
    attn_gain,
    w_query,
    key_weight,
    value_weight,
    w_out,
    mlp_gain,
    gate_weight,
    up_weight,
    down_weight,
    cotangent,
):
    devices = lax.axis_size("fsdp")
    rows, ff = gate_weight.shape[1:]
    width = rows * devices
    kv = key_weight.shape[2]
    down_rows = down_weight.shape[1]
    layouts = [geometry(piece) for piece in blocks_of(segment)]
    layout = ([item[0] for item in layouts],) + tuple(
        jnp.concatenate([item[member] for item in layouts]) for member in range(1, 4)
    )
    active_rows = layout[1]

    all_gains = jnp.concatenate([attn_gain, mlp_gain]).reshape(1, 4 * rows)
    all_gains = jnp.pad(all_gains, ((0, 0), (0, 2 * width + 2 * kv - 4 * rows)))
    attn_weights, feed_weights = [], []
    gains = None
    for layer in range(DECODER_LAYERS):
        packed = jnp.concatenate(
            [w_query[layer], key_weight[layer], value_weight[layer], w_out[layer]], axis=1
        )
        if layer == 0:
            packed = jnp.concatenate([packed, all_gains])
        whole = lax.all_gather(packed, "fsdp", axis=0, tiled=False)
        if layer == 0:
            gains = whole[:, rows, : 4 * rows].reshape(devices, 4, rows)
            gains = gains.transpose(1, 0, 2).reshape(4, width).astype(jnp.float32)
        whole = whole[:, :rows].reshape(width, -1)
        attn_weights.append(
            (
                whole[:, :width],
                whole[:, width : width + kv],
                whole[:, width + kv : width + 2 * kv],
                whole[:, width + 2 * kv :],
            )
        )
        packed = jnp.concatenate(
            [gate_weight[layer], up_weight[layer], down_weight[layer].reshape(rows, ff)]
        )
        whole = lax.all_gather(packed, "fsdp", axis=0, tiled=False)
        feed_weights.append(
            (
                whole[:, :rows].reshape(width, ff),
                whole[:, rows : 2 * rows].reshape(width, ff),
                whole[:, 2 * rows :].reshape(ff, width),
            )
        )

    residual = tokens.astype(jnp.float32)
    saved = []
    for layer in range(DECODER_LAYERS):
        residual, kept = layer_forward(
            residual,
            attn_weights[layer],
            feed_weights[layer],
            (gains[layer], gains[DECODER_LAYERS + layer]),
            layout,
        )
        saved.append(kept)
    out_tokens = residual.astype(jnp.bfloat16)

    upstream = cotangent.astype(jnp.float32)
    shards = [None] * DECODER_LAYERS
    for layer in reversed(range(DECODER_LAYERS)):
        grad_hidden, mlp_gain_grad, feed_grads = feed_backward(
            saved[layer],
            feed_weights[layer],
            gains[DECODER_LAYERS + layer],
            active_rows,
            upstream,
        )
        buffer = jnp.concatenate(
            [
                feed_grads[0].reshape(devices, rows, ff),
                feed_grads[1].reshape(devices, rows, ff),
                feed_grads[2].reshape(devices, rows, ff),
            ],
            axis=1,
        )
        feed_shard = sum_shards(buffer, False)
        upstream, attn_gain_grad, attn_grads = attention_part_backward(
            saved[layer], attn_weights[layer], gains[layer], layout, grad_hidden
        )
        gain_grads = jnp.concatenate(
            [attn_gain_grad.reshape(devices, rows), mlp_gain_grad.reshape(devices, rows)], axis=1
        ).astype(jnp.bfloat16)
        gain_grads = jnp.pad(gain_grads, ((0, 0), (0, 2 * width + 2 * kv - 2 * rows)))
        buffer = jnp.concatenate(
            [
                jnp.concatenate(attn_grads, axis=1).reshape(devices, rows, -1),
                gain_grads[:, None],
            ],
            axis=1,
        )
        attn_shard = sum_shards(buffer, layer == 0)
        feed_shard = feed_shard.astype(jnp.float32)
        attn_shard = attn_shard.astype(jnp.float32)
        block = attn_shard[:rows]
        shards[layer] = (
            attn_shard[rows, :rows],
            block[:, :width],
            block[:, width : width + kv],
            block[:, width + kv : width + 2 * kv],
            block[:, width + 2 * kv :],
            attn_shard[rows, rows : 2 * rows],
            feed_shard[:rows],
            feed_shard[rows : 2 * rows],
            feed_shard[2 * rows : 3 * rows].reshape(down_rows, width),
        )
    stacked = tuple(
        jnp.stack([shards[layer][member] for layer in range(DECODER_LAYERS)])
        for member in range(9)
    )
    return (out_tokens, upstream) + stacked


def solution(mesh):
    in_specs = (
        P(("rep", "fsdp"), None),
        P(("rep", "fsdp")),
        P(None, "fsdp"),
        P(None, "fsdp", None),
        P(None, "fsdp", None),
        P(None, "fsdp", None),
        P(None, "fsdp", None),
        P(None, "fsdp"),
        P(None, "fsdp", None),
        P(None, "fsdp", None),
        P(None, "fsdp", None),
        P(("rep", "fsdp"), None),
    )
    out_specs = (
        P(("rep", "fsdp"), None),
        P(("rep", "fsdp"), None),
        P(None, "fsdp"),
        P(None, "fsdp", None),
        P(None, "fsdp", None),
        P(None, "fsdp", None),
        P(None, "fsdp", None),
        P(None, "fsdp"),
        P(None, "fsdp", None),
        P(None, "fsdp", None),
        P(None, "fsdp", None),
    )
    return jax.shard_map(local, mesh=mesh, in_specs=in_specs, out_specs=out_specs, check_vma=False)
```

time: 1190 us -> 828 us (0.70)
  waiting for transfers between devices: 355 us -> 190 us
  matrix products: 467 us -> 318 us
  blocking collectives: 169 us -> 60.8 us
  local copies, waits for them, and re-layouts: 46.8 us -> 98.8 us
    dot_general x120 -> x66, matrix products: 467 us -> 318 us  [the longest x14 58.8 us: contract_rows(): lax.dot_general(left, right, (((0,), (0,)), ((), ())), preferred_element_...]
    psum x2 -> x0, waiting for transfers between devices: 104 us -> none  [the longest x1 65.7 us: local(): lax.psum(shards[1].astype(jnp.bfloat16), 'rep').astype(jnp.float32)]
    all_gather x8 -> x3, blocking collectives: 135 us -> 31.4 us  [sum_shards(): return lax.all_gather(part, 'rep', axis=0, tiled=True)]
    reduce_scatter x10 -> x4, waiting for transfers between devices: 214 us -> 112 us  [sum_shards(): shard = lax.psum_scatter(buffer, 'fsdp', scatter_dimension=0, tiled=False)]
    all_gather x6 -> x4, waiting for transfers between devices: 0.01 us -> 76.7 us  [local(): whole = lax.all_gather(packed, 'fsdp', axis=0, tiled=False)]
    unnamed x26 -> x12, waiting for transfers between devices: 36.4 us -> 1.97 us
    reshape x0 -> x9, local copies, waits for them, and re-layouts: none -> 30.1 us  [the longest x2 19.5 us: local(): whole[:, 2 * rows:].reshape(ff, width)]
    unnamed x523 -> x216, local copies, waits for them, and re-layouts: 39.7 us -> 23.7 us
  transfers between devices with their start and end apart: 22 -> 11, of which waited for: 10 -> 7; matrix products, arithmetic and copies ran while one was open for 32% -> 27% of each run, Pallas kernels for 0% -> 0%
where the time goes in v1:
time: 828 us; the launch traced here: 822 us
  matrix products  318 us (38%)
  waiting for transfers between devices  190 us (23%)
  other arithmetic  130 us (16%)
  local copies, waits for them, and re-layouts  98.8 us (12%)
  blocking collectives  60.8 us (7%)
  between operations  17 us (2%)
    reduce_scatter x4, waiting for transfers between devices, sum_shards(): shard = lax.psum_scatter(buffer, 'fsdp', scatter_dimension=0, tiled=False)  112 us
    all_gather x4, waiting for transfers between devices, local(): whole = lax.all_gather(packed, 'fsdp', axis=0, tiled=False)  76.7 us
    dot_general x14, matrix products, contract_rows(): lax.dot_general(left, right, (((0,), (0,)), ((), ())), preferred_element_...  58.8 us
    convert_element_type x4, other arithmetic, attention_backward(): grad_scores = (probs_full * (grad_probs - row_weight)).astype(jnp.bfloat16)  56.9 us
    dot_general x4, matrix products, attention_backward(): jnp.einsum('qgjd,kgd->gjqk', mixed_gradient, values, preferred_element_ty...  53.3 us
    dot_general x14, matrix products, times_transposed(): lax.dot_general(left, right, (((1,), (1,)), ((), ())), preferred_element_...  50.2 us
    dot_general x4, matrix products, attention_backward(): jnp.einsum('gjqk,qgjd->kgd', probs, mixed_gradient, preferred_element_typ...  37.1 us
    all_gather x3, blocking collectives, sum_shards(): return lax.all_gather(part, 'rep', axis=0, tiled=True)  31.4 us
  transfers between devices with their start and end apart: 11, of which 7 were waited for; matrix products, arithmetic and copies ran while one was open for 27% of the time, Pallas kernels for 0%

profile of v1, /device:TPU:0, one launch (start us, length us, event | category | flops | bytes accessed | tf_op | source)
XLA Modules:
  0.0 822.4 jit_solution(9073908762204873492)
XLA Ops:
  20.9 20.9 %all-gather.19.cloned.1.call-done = bf16[8,73,1536]{2,1,0:T(8,128)(2,1)} async-done(((bf16[1,73,1536]{2,1,0:T(8,128)(2,1)}), bf16[8,73,1536]{2,1,0:T(8,128)(2,1)}) %all-gather.19.cloned.1.call-update) | async-done | bytes 1794064 | tf_op jit(solution)/shard_map/all_gather | solution.py:308
  93.3 6.9 all-gather.17.cloned.1.call-done
  108.8 49.0 %all-gather.13.cloned.1.call-done = bf16[1728,1536]{1,0:T(8,128)(2,1)} async-done(((bf16[216,1536]{1,0:T(8,128)(2,1)}), bf16[1728,1536]{1,0:T(8,128)(2,1)}) %all-gather.13.cloned.1.call-update) | async-done | bytes 5308432 | tf_op jit(solution)/shard_map/all_gather | solution.py:324
  162.5 15.6 %reshape.552 = bf16[1536,576]{1,0:T(8,128)(2,1)} reshape(bf16[8,72,1536]{2,1,0:T(8,128)(2,1)S(1)} %get-tuple-element.37) | data formatting | bytes 3538944 | tf_op jit(solution)/shard_map/reshape | solution.py:329
  183.7 7.4 multiply_convert_fusion.1
  248.1 6.5 fusion.193
  254.5 15.1 %fusion.40 = (bf16[1536,1536]{1,0:T(8,128)(2,1)}, bf16[1536,1536]{1,0:T(8,128)(2,1)}, bf16[1536,1536]{1,0:T(8,128)(2,1)}) fusion(bf16[1536,1536]{1,0:T(8,128)(2,1)} %convolution_convert_fusion.1, f32[1536,1536]{1,0:T(8,128)} %fusion.193, bf16[1536,576]{0,1:T(8,128)(2,1)S(1)} %multiply_convert_fusion.5, bf16[576,1536]{1,0:T(8,128)(2,1)S(1)} %bitcast.417), kind=kOutput, calls=%fused_computation.62 | convolution fusion | flops 2755657728 | bytes 31850496 | tf_op jit(solution)/shard_map/dot_general | solution.py:149
  284.3 9.0 %fusion.92 = bf16[3,64,768]{2,1,0:T(8,128)(2,1)S(1)} fusion(bf16[768,3,3,64]{0,3,2,1:T(8,128)(2,1)S(1)} %bitcast.379, f32[3,3,768,768]{2,3,1,0:T(8,128)} %copy-done.3, f32[3,3,768]{2,1,0:T(4,128)S(1)} %log_add_fusion.2), kind=kOutput, calls=%fused_computation.194 | convolution fusion | flops 690241536 | bytes 22440960 | tf_op jit(solution)/shard_map/gjqk,qgjd->kgd/dot_general | solution.py:102
  293.4 13.3 %fusion.11 = (f32[3,3,768]{2,1,0:T(4,128)S(1)}, f32[3,768,768,3]{2,1,3,0:T(8,128)}) fusion(f32[3,3,768,768]{2,3,1,0:T(8,128)} %copy-done.3, f32[3,3,768]{2,1,0:T(4,128)S(1)} %log_add_fusion.2, bf16[768,3,64,1]{0,2,3,1:T(8,128)(2,1)S(1)} %bitcast.441, bf16[768,3,3,64]{0,3,2,1:T(8,128)(2,1)S(1)} %bitcast.380), kind=kOutput, calls=%fused_computation.17 | convolution fusion | flops 695395584 | bytes 43702272 | tf_op jit(solution)/shard_map/qgjd,kgd->gjqk/dot_general | solution.py:105
  306.7 14.1 %fusion.13 = bf16[3,3,768,768]{2,3,1,0:T(8,128)(2,1)S(1)} fusion(f32[3,768,768,3]{2,1,3,0:T(8,128)} %get-tuple-element.140, f32[3,3,768,768]{2,3,1,0:T(8,128)} %copy-done.3, f32[3,3,768]{2,1,0:T(4,128)S(1)} %get-tuple-element.139, f32[3,3,768]{2,1,0:T(4,128)S(1)} %log_add_fusion.2), kind=kLoop, calls=%fused_computation.19 | loop fusion | flops 21233664 | bytes 53139456 | tf_op jit(solution)/shard_map/convert_element_type | solution.py:109
  326.1 8.8 %fusion.89 = bf16[3,64,768]{2,1,0:T(8,128)(2,1)S(1)} fusion(bf16[768,3,3,64]{0,3,2,1:T(8,128)(2,1)S(1)} %bitcast.375, f32[3,3,768,768]{2,3,1,0:T(8,128)} %copy-done.1, f32[3,3,768]{2,1,0:T(4,128)S(1)} %copy-done.68), kind=kOutput, calls=%fused_computation.193 | convolution fusion | flops 690241536 | bytes 22440960 | tf_op jit(solution)/shard_map/gjqk,qgjd->kgd/dot_general | solution.py:102
  334.9 13.4 %fusion.8 = (f32[3,3,768]{2,1,0:T(4,128)S(1)}, f32[3,768,768,3]{2,1,3,0:T(8,128)}) fusion(f32[3,3,768,768]{2,3,1,0:T(8,128)} %copy-done.1, f32[3,3,768]{2,1,0:T(4,128)S(1)} %copy-done.68, bf16[768,3,64,1]{0,2,3,1:T(8,128)(2,1)S(1)} %bitcast.439, bf16[768,3,3,64]{0,3,2,1:T(8,128)(2,1)S(1)} %bitcast.376), kind=kOutput, calls=%fused_computation.12 | convolution fusion | flops 695395584 | bytes 43702272 | tf_op jit(solution)/shard_map/qgjd,kgd->gjqk/dot_general | solution.py:105
  348.3 14.6 %fusion.10 = bf16[3,3,768,768]{2,3,1,0:T(8,128)(2,1)S(1)} fusion(f32[3,768,768,3]{2,1,3,0:T(8,128)} %get-tuple-element.138, f32[3,3,768,768]{2,3,1,0:T(8,128)} %copy-done.1, f32[3,3,768]{2,1,0:T(4,128)S(1)} %get-tuple-element.137, f32[3,3,768]{2,1,0:T(4,128)S(1)} %copy-done.68), kind=kLoop, calls=%fused_computation.14 | loop fusion | flops 21233664 | bytes 53139456 | tf_op jit(solution)/shard_map/convert_element_type | solution.py:109
  380.9 14.7 %fusion.45 = (bf16[1536,1536]{1,0:T(8,128)(2,1)}, bf16[1536,1536]{1,0:T(8,128)(2,1)}) fusion(f32[1536,1536]{1,0:T(8,128)} %copy-done.102, f32[1536,1536]{1,0:T(8,128)} %get-tuple-element.127, bf16[1536,576]{1,0:T(8,128)(2,1)S(1)} %copy-done.42, f32[1536,576]{0,1:T(8,128)S(1)} %subtract_add_fusion.1, f32[1536]{0:T(1024)S(1)} %maximum_reduce_fusion), kind=kOutput, calls=%fused_computation.67 | convolution fusion | flops 2755067904 | bytes 33626112 | tf_op jit(solution)/shard_map/dot_general | solution.py:181
  408.5 9.5 %fusion.95 = bf16[3,64,768]{2,1,0:T(8,128)(2,1)} fusion(bf16[768,3,3,64]{0,3,2,1:T(8,128)(2,1)S(1)} %bitcast.381, f32[3,3,768,768]{2,3,1,0:T(8,128)} %copy-done.2, f32[3,3,768]{2,1,0:T(4,128)S(1)} %copy-done.67), kind=kOutput, calls=%fused_computation.195 | convolution fusion | flops 690241536 | bytes 22440960 | tf_op jit(solution)/shard_map/gjqk,qgjd->kgd/dot_general | solution.py:102
  418.0 13.3 %fusion.5 = (f32[3,3,768]{2,1,0:T(4,128)S(1)}, f32[3,768,768,3]{2,1,3,0:T(8,128)}) fusion(f32[3,3,768,768]{2,3,1,0:T(8,128)} %copy-done.2, f32[3,3,768]{2,1,0:T(4,128)S(1)} %copy-done.67, bf16[768,3,64,1]{0,2,3,1:T(8,128)(2,1)S(1)} %bitcast.437, bf16[768,3,3,64]{0,3,2,1:T(8,128)(2,1)S(1)} %bitcast.382), kind=kOutput, calls=%fused_computation.7 | convolution fusion | flops 695395584 | bytes 43702272 | tf_op jit(solution)/shard_map/qgjd,kgd->gjqk/dot_general | solution.py:105
  431.3 14.1 %fusion.7 = bf16[3,3,768,768]{2,3,1,0:T(8,128)(2,1)S(1)} fusion(f32[3,768,768,3]{2,1,3,0:T(8,128)} %get-tuple-element.146, f32[3,3,768,768]{2,3,1,0:T(8,128)} %copy-done.2, f32[3,3,768]{2,1,0:T(4,128)S(1)} %get-tuple-element.145, f32[3,3,768]{2,1,0:T(4,128)S(1)} %copy-done.67), kind=kLoop, calls=%fused_computation.9 | loop fusion | flops 21233664 | bytes 53139456 | tf_op jit(solution)/shard_map/convert_element_type | solution.py:109
  452.1 9.7 %fusion.86 = bf16[3,64,768]{2,1,0:T(8,128)(2,1)} fusion(bf16[768,3,3,64]{0,3,2,1:T(8,128)(2,1)S(1)} %bitcast.377, f32[3,3,768,768]{2,3,1,0:T(8,128)} %copy-done, f32[3,3,768]{2,1,0:T(4,128)S(1)} %copy-done.66), kind=kOutput, calls=%fused_computation.192 | convolution fusion | flops 690241536 | bytes 22440960 | tf_op jit(solution)/shard_map/gjqk,qgjd->kgd/dot_general | solution.py:102
  461.8 13.3 %fusion.2 = (f32[3,3,768]{2,1,0:T(4,128)S(1)}, f32[3,768,768,3]{2,1,3,0:T(8,128)}) fusion(f32[3,3,768,768]{2,3,1,0:T(8,128)} %copy-done, f32[3,3,768]{2,1,0:T(4,128)S(1)} %copy-done.66, bf16[768,3,64,1]{0,2,3,1:T(8,128)(2,1)S(1)} %bitcast.435, bf16[768,3,3,64]{0,3,2,1:T(8,128)(2,1)S(1)} %bitcast.378), kind=kOutput, calls=%fused_computation.2 | convolution fusion | flops 695395584 | bytes 43702272 | tf_op jit(solution)/shard_map/qgjd,kgd->gjqk/dot_general | solution.py:105
  475.1 14.1 %fusion.4 = bf16[3,3,768,768]{2,3,1,0:T(8,128)(2,1)S(1)} fusion(f32[3,768,768,3]{2,1,3,0:T(8,128)} %get-tuple-element.144, f32[3,3,768,768]{2,3,1,0:T(8,128)} %copy-done, f32[3,3,768]{2,1,0:T(4,128)S(1)} %get-tuple-element.143, f32[3,3,768]{2,1,0:T(4,128)S(1)} %copy-done.66), kind=kLoop, calls=%fused_computation.4 | loop fusion | flops 21233664 | bytes 53139456 | tf_op jit(solution)/shard_map/convert_element_type | solution.py:109
  534.2 7.0 convolution_convert_fusion.2
  550.2 7.2 convolution_convert_fusion.7
  557.5 6.4 convolution_convert_fusion.6
  565.6 8.4 %reduce-scatter.9.cloned.1.call-done = bf16[1,73,1536]{2,1,0:T(8,128)(2,1)} async-done(((bf16[8,73,1536]{2,1,0:T(8,128)(2,1)}), bf16[1,73,1536]{2,1,0:T(8,128)(2,1)}) %reduce-scatter.9.cloned.1.call-update) | async-done | bytes 224272 | tf_op jit(solution)/shard_map/reduce_scatter | solution.py:261
  580.2 7.7 convolution_convert_fusion.3
  620.1 6.5 add_convert_fusion
  627.5 9.1 %all-gather.5 = bf16[4,19,1536]{2,1,0:T(8,128)(2,1)S(1)} all-gather(bf16[1,19,1536]{2,1,0:T(8,128)(2,1)S(1)} %dynamic-slice_bitcast_fusion.2), channel_id=1, replica_groups=mesh['rep'=4,'fsdp'=8] {'rep'}, dimensions={0}, use_global_device_ids=true | all-gather | bytes 291840 | tf_op jit(solution)/shard_map/all_gather | solution.py:270
  642.5 41.8 %reduce-scatter.15.cloned.1.call-done = bf16[1,216,1536]{2,1,0:T(8,128)(2,1)} async-done(((bf16[8,216,1536]{2,1,0:T(8,128)(2,1)}), bf16[1,216,1536]{2,1,0:T(8,128)(2,1)}) %reduce-scatter.15.cloned.1.call-update) | async-done | bytes 663568 | tf_op jit(solution)/shard_map/reduce_scatter | solution.py:261
  684.3 61.4 %reduce-scatter.13.cloned.1.call-done = bf16[1,216,1536]{2,1,0:T(8,128)(2,1)} async-done(((bf16[8,216,1536]{2,1,0:T(8,128)(2,1)}), bf16[1,216,1536]{2,1,0:T(8,128)(2,1)}) %reduce-scatter.13.cloned.1.call-update) | async-done | bytes 663568 | tf_op jit(solution)/shard_map/reduce_scatter | solution.py:261
  745.6 29.4 %fusion.174 = (bf16[64,1536]{1,0:T(8,128)(2,1)S(1)}, bf16[64,1536]{1,0:T(8,128)(2,1)S(1)}) fusion(bf16[216,1536]{1,0:T(8,128)(2,1)} %bitcast.442, bf16[216,1536]{1,0:T(8,128)(2,1)} %bitcast.443), kind=kCustom, calls=%all-reduce-scatter.2 | all-reduce-scatter fusion | flops 786433 | bytes 1720832
  784.6 12.8 %all-gather.7 = bf16[4,54,1536]{2,1,0:T(8,128)(2,1)S(1)} all-gather(bf16[1,54,1536]{2,1,0:T(8,128)(2,1)S(1)} %dynamic-slice_bitcast_fusion), channel_id=1, replica_groups=mesh['rep'=4,'fsdp'=8] {'rep'}, dimensions={0}, use_global_device_ids=true | all-gather | bytes 829440 | tf_op jit(solution)/shard_map/all_gather | solution.py:270
  797.3 9.5 %all-gather.6 = bf16[4,54,1536]{2,1,0:T(8,128)(2,1)S(1)} all-gather(bf16[1,54,1536]{2,1,0:T(8,128)(2,1)S(1)} %dynamic-slice_bitcast_fusion.1), channel_id=1, replica_groups=mesh['rep'=4,'fsdp'=8] {'rep'}, dimensions={0}, use_global_device_ids=true | all-gather | bytes 829440 | tf_op jit(solution)/shard_map/all_gather | solution.py:270
  (415 shorter events, 314.7 us)
Async XLA Ops:
  7.2 34.5 %all-gather.19.cloned.1.call-start = ((), (), s32[]{:S(2)}) async-start(), calls=%async_computation.11 | async-start | bytes 2211840 | tf_op jit(solution)/shard_map/all_gather | solution.py:308
  10.9 89.3 %all-gather.17.cloned.1.call-start = ((), (), s32[]{:S(2)}) async-start(), calls=%async_computation.10 | async-start | bytes 5971968 | tf_op jit(solution)/shard_map/all_gather | solution.py:324
  13.4 144.3 %all-gather.13.cloned.1.call-start = ((), (), s32[]{:S(2)}) async-start(), calls=%async_computation.8 | async-start | bytes 5971968 | tf_op jit(solution)/shard_map/all_gather | solution.py:324
  14.8 183.8 %all-gather.15.cloned.1.call-start = ((), (), s32[]{:S(2)}) async-start(), calls=%async_computation.9 | async-start | bytes 1990656 | tf_op jit(solution)/shard_map/all_gather | solution.py:308
  15.7 548.3 %reduce-scatter.11.cloned.1.call-start = ((), (), s32[]{:S(2)}) async-start(), calls=%async_computation.5 | async-start | bytes 2211840 | tf_op jit(solution)/shard_map/reduce_scatter | solution.py:261
  19.0 38.8 %copy-start.6 = (pred[768,768]{0,1:T(8,128)(4,1)}, pred[768,768]{0,1:T(8,128)(4,1)S(1)}, u32[]{:S(2)}) copy-start(pred[768,768]{0,1:T(8,128)(4,1)S(1)} %get-tuple-element.152) | copy-start | bytes 1769476
  20.0 27.8 %copy-start.81 = (f32[1536]{0:T(1024)}, f32[1536]{0:T(1024)S(1)}, u32[]{:S(2)}) copy-start(f32[1536]{0:T(1024)S(1)} %get-tuple-element.101) | copy-start | bytes 18436
  20.8 34.1 %copy-start.8 = (f32[1536,32]{0,1:T(8,128)}, f32[1536,32]{0,1:T(8,128)S(1)}, u32[]{:S(2)}) copy-start(f32[1536,32]{0,1:T(8,128)S(1)} %maximum_bitcast_fusion) | copy-start | bytes 589828
  20.9 34.1 %copy-start.11 = (f32[1536,32]{0,1:T(8,128)}, f32[1536,32]{0,1:T(8,128)S(1)}, u32[]{:S(2)}) copy-start(f32[1536,32]{0,1:T(8,128)S(1)} %maximum_bitcast_fusion.1) | copy-start | bytes 589828
  52.0 143.9 %copy-start.83 = (f32[576]{0:T(1024)}, f32[576]{0:T(1024)S(1)}, u32[]{:S(2)}) copy-start(f32[576]{0:T(1024)S(1)} %mul.804) | copy-start | bytes 6916
  52.1 39.7 %copy-start.88 = (f32[576]{0:T(1024)}, f32[576]{0:T(1024)S(1)}, u32[]{:S(2)}) copy-start(f32[576]{0:T(1024)S(1)} %mul.795) | copy-start | bytes 6916
  53.3 12.8 %copy-start.58 = (bf16[768,192]{0,1:T(8,128)(2,1)}, bf16[768,192]{0,1:T(8,128)(2,1)S(1)}, u32[]{:S(2)}) copy-start(bf16[768,192]{0,1:T(8,128)(2,1)S(1)} %get-tuple-element.73) | copy-start | bytes 884740
  53.3 27.7 %copy-start.60 = (bf16[768,192]{0,1:T(8,128)(2,1)}, bf16[768,192]{0,1:T(8,128)(2,1)S(1)}, u32[]{:S(2)}) copy-start(bf16[768,192]{0,1:T(8,128)(2,1)S(1)} %get-tuple-element.72) | copy-start | bytes 884740
  54.9 17.9 %copy-start.30 = (bf16[1536,3,32]{0,2,1:T(8,128)(2,1)}, bf16[1536,3,32]{0,2,1:T(8,128)(2,1)S(1)}, u32[]{:S(2)}) copy-start(bf16[1536,3,32]{0,2,1:T(8,128)(2,1)S(1)} %get-tuple-element.62) | copy-start | bytes 884740
  54.9 17.9 %copy-start.32 = (bf16[1536,3,32]{0,2,1:T(8,128)(2,1)}, bf16[1536,3,32]{0,2,1:T(8,128)(2,1)S(1)}, u32[]{:S(2)}) copy-start(bf16[1536,3,32]{0,2,1:T(8,128)(2,1)S(1)} %get-tuple-element.63) | copy-start | bytes 884740
  57.8 15.0 %copy-start.34 = (bf16[768,9,64]{0,2,1:T(8,128)(2,1)}, bf16[768,9,64]{0,2,1:T(8,128)(2,1)S(1)}, u32[]{:S(2)}) copy-start(bf16[768,9,64]{0,2,1:T(8,128)(2,1)S(1)} %get-tuple-element.54) | copy-start | bytes 2654212
  72.8 14.8 %copy-start.96 = (bf16[3,64,3,768]{3,1,2,0:T(8,128)(2,1)}, bf16[3,64,3,768]{3,1,2,0:T(8,128)(2,1)S(1)}, u32[]{:S(2)}) copy-start(bf16[3,64,3,768]{3,1,2,0:T(8,128)(2,1)S(1)} %fusion.64) | copy-start | bytes 2654212
  93.3 90.4 %copy-start.44 = (bf16[1536,576]{0,1:T(8,128)(2,1)}, bf16[1536,576]{0,1:T(8,128)(2,1)S(1)}, u32[]{:S(2)}) copy-start(bf16[1536,576]{0,1:T(8,128)(2,1)S(1)} %multiply_convert_fusion.7) | copy-start | bytes 5308420
  195.2 41.4 %copy-start.4 = (f32[1536,576]{0,1:T(8,128)}, f32[1536,576]{0,1:T(8,128)S(1)}, u32[]{:S(2)}) copy-start(f32[1536,576]{0,1:T(8,128)S(1)} %get-tuple-element.129) | copy-start | bytes 10616836
  240.4 38.2 %copy-start.20 = (f32[1536,576]{0,1:T(8,128)}, f32[1536,576]{0,1:T(8,128)S(1)}, u32[]{:S(2)}) copy-start(f32[1536,576]{0,1:T(8,128)S(1)} %get-tuple-element.135) | copy-start | bytes 10616836
  348.3 14.6 %copy-start.28 = (bf16[768,9,64]{0,2,1:T(8,128)(2,1)S(1)}, bf16[768,9,64]{0,2,1:T(8,128)(2,1)}, u32[]{:S(2)}) copy-start(bf16[768,9,64]{0,2,1:T(8,128)(2,1)} %copy-done.27) | copy-start | bytes 2654212
  380.2 24.2 %copy-start.19 = (f32[1536,576]{0,1:T(8,128)}, f32[1536,576]{0,1:T(8,128)S(1)}, u32[]{:S(2)}) copy-start(f32[1536,576]{0,1:T(8,128)S(1)} %subtract_add_fusion.1) | copy-start | bytes 10616836
  380.9 14.7 %copy-start.52 = (bf16[8,72,1536]{2,1,0:T(8,128)(2,1)S(1)}, bf16[8,72,1536]{2,1,0:T(8,128)(2,1)}, u32[]{:S(2)}) copy-start(bf16[8,72,1536]{2,1,0:T(8,128)(2,1)} %get-tuple-element.39) | copy-start | bytes 5308420
  431.3 14.2 %copy-start.35 = (bf16[768,9,64]{0,2,1:T(8,128)(2,1)S(1)}, bf16[768,9,64]{0,2,1:T(8,128)(2,1)}, u32[]{:S(2)}) copy-start(bf16[768,9,64]{0,2,1:T(8,128)(2,1)} %copy-done.34) | copy-start | bytes 2654212
  452.1 9.7 %copy-start.59 = (bf16[768,192]{0,1:T(8,128)(2,1)S(1)}, bf16[768,192]{0,1:T(8,128)(2,1)}, u32[]{:S(2)}) copy-start(bf16[768,192]{0,1:T(8,128)(2,1)} %copy-done.58) | copy-start | bytes 884740
  475.1 14.2 %copy-start.26 = (bf16[768,9,64]{0,2,1:T(8,128)(2,1)S(1)}, bf16[768,9,64]{0,2,1:T(8,128)(2,1)}, u32[]{:S(2)}) copy-start(bf16[768,9,64]{0,2,1:T(8,128)(2,1)} %copy-done.25) | copy-start | bytes 2654212
  503.5 70.5 %reduce-scatter.9.cloned.1.call-start = ((), (), s32[]{:S(2)}) async-start(), calls=%async_computation.4 | async-start | bytes 2211840 | tf_op jit(solution)/shard_map/reduce_scatter | solution.py:261
  534.2 92.4 %all-reduce.13.cloned.1.call-start = ((), (), s32[]{:S(2)}) async-start(), calls=%async_computation.12 | async-start | bytes 983040
  574.0 110.2 %reduce-scatter.15.cloned.1.call-start = ((), (), s32[]{:S(2)}) async-start(), calls=%async_computation.7 | async-start | bytes 5971968 | tf_op jit(solution)/shard_map/reduce_scatter | solution.py:261
  579.9 165.7 %reduce-scatter.13.cloned.1.call-start = ((), (), s32[]{:S(2)}) async-start(), calls=%async_computation.6 | async-start | bytes 5971968 | tf_op jit(solution)/shard_map/reduce_scatter | solution.py:261
  775.1 7.0 collective-permute-start
  778.7 5.5 collective-permute-start.1
  (83 other events, 333.7 us)
Sparse Core Ops, SparseCore 0:
  11.0 30.7 all-gather.18
  43.9 56.1 all-gather.16
  102.4 55.3 all-gather.12
  159.8 25.1 all-gather.14
  503.6 34.2 reduce-scatter.10
  540.2 33.7 reduce-scatter.8
  577.6 43.6 all-reduce.12
  623.7 60.5 reduce-scatter.14
  686.7 58.8 reduce-scatter.12

commit v2 on v1

--- a/solution.py
+++ b/solution.py
@@ -1,6 +1,8 @@
 import jax
 import jax.numpy as jnp
 from jax import lax
+from jax.experimental import pallas as pl
+from jax.experimental.pallas import tpu as pltpu
 from jax.sharding import PartitionSpec as P
 
 QUERY_HEADS = 9
@@ -67,57 +69,154 @@
     return (through, jnp.sum(upstream * value_rows * factor, axis=0))
 
 
-def attention_forward(query_rows, key_rows, value_rows, allowed):
+def row_tile(count_of_rows):
+    return 256 if count_of_rows % 256 == 0 else count_of_rows
+
+
+def tile_mask(column_ref, row_ref, start, size):
+    reach = start + size
+    shape = (size, reach)
+    row_number = lax.broadcasted_iota(jnp.int32, shape, 0) + start
+    key_number = lax.broadcasted_iota(jnp.int32, shape, 1)
+    same = column_ref[start : start + size, :] == row_ref[0, :, :reach]
+    allowed = jnp.where(same & (key_number <= row_number), 1.0, 0.0)
+    return jnp.concatenate([allowed] * (QUERY_HEADS // KEY_VALUE_HEADS), axis=0) > 0.5
+
+
+def head_stack(ref, start, size, group):
+    heads = QUERY_HEADS // KEY_VALUE_HEADS
+    first = group * heads * HEAD_WIDTH
+    piece = ref[start : start + size, first : first + heads * HEAD_WIDTH]
+    return jnp.concatenate(
+        [piece[:, j * HEAD_WIDTH : (j + 1) * HEAD_WIDTH] for j in range(heads)], axis=0
+    )
+
+
+def head_unstack(stacked, size):
+    heads = QUERY_HEADS // KEY_VALUE_HEADS
+    return [stacked[j * size : (j + 1) * size] for j in range(heads)]
+
+
+def dot_rows(left, right):
+    return lax.dot_general(
+        left, right, (((0,), (0,)), ((), ())), preferred_element_type=jnp.float32
+    )
+
+
+def forward_kernel(column_ref, row_ref, query_ref, key_ref, value_ref, mixed_ref, total_ref):
+    count_of_rows = query_ref.shape[0]
+    size = row_tile(count_of_rows)
+    scale = HEAD_WIDTH ** (-0.5)
+    for start in range(0, count_of_rows, size):
+        reach = start + size
+        allowed = tile_mask(column_ref, row_ref, start, size)
+        outputs, totals = [], []
+        for group in range(KEY_VALUE_HEADS):
+            lanes = slice(group * HEAD_WIDTH, (group + 1) * HEAD_WIDTH)
+            queries = head_stack(query_ref, start, size, group)
+            scores = times_transposed(queries, key_ref[:reach, lanes]) * scale
+            scores = jnp.where(allowed, scores, masked_fill)
+            peak = jnp.max(scores, axis=-1, keepdims=True)
+            expo = jnp.exp(scores - peak)
+            total = jnp.sum(expo, axis=-1, keepdims=True)
+            probs = (expo * (1.0 / total)).astype(jnp.bfloat16)
+            mixed = jnp.dot(probs, value_ref[:reach, lanes], preferred_element_type=jnp.float32)
+            outputs += head_unstack(mixed, size)
+            totals += head_unstack(peak + jnp.log(total), size)
+        mixed_ref[start:reach, :] = jnp.concatenate(outputs, axis=1).astype(jnp.bfloat16)
+        total_ref[start:reach, :] = jnp.concatenate(totals, axis=1)
+
+
+def backward_kernel(
+    column_ref,
+    row_ref,
+    query_ref,
+    key_ref,
+    value_ref,
+    total_ref,
+    upstream_ref,
+    grad_query_ref,
+    grad_key_ref,
+    grad_value_ref,
+):
+    count_of_rows = query_ref.shape[0]
+    size = row_tile(count_of_rows)
+    scale = HEAD_WIDTH ** (-0.5)
+    heads = QUERY_HEADS // KEY_VALUE_HEADS
+    for start in reversed(range(0, count_of_rows, size)):
+        reach = start + size
+        allowed = tile_mask(column_ref, row_ref, start, size)
+        query_grads, key_grads, value_grads = [], [], []
+        for group in range(KEY_VALUE_HEADS):
+            lanes = slice(group * HEAD_WIDTH, (group + 1) * HEAD_WIDTH)
+            queries = head_stack(query_ref, start, size, group)
+            upstream = head_stack(upstream_ref, start, size, group)
+            keys = key_ref[:reach, lanes]
+            values = value_ref[:reach, lanes]
+            totals = total_ref[start:reach, :]
+            total = jnp.concatenate(
+                [totals[:, group * heads + j : group * heads + j + 1] for j in range(heads)], axis=0
+            )
+            scores = times_transposed(queries, keys) * scale
+            scores = jnp.where(allowed, scores, masked_fill)
+            probs_full = jnp.exp(scores - total)
+            value_grads.append(dot_rows(probs_full.astype(jnp.bfloat16), upstream))
+            grad_probs = times_transposed(upstream, values)
+            row_weight = jnp.sum(probs_full * grad_probs, axis=-1, keepdims=True)
+            grad_scores = (probs_full * (grad_probs - row_weight)).astype(jnp.bfloat16)
+            grad_queries = jnp.dot(grad_scores, keys, preferred_element_type=jnp.float32) * scale
+            query_grads += head_unstack(grad_queries, size)
+            key_grads.append(dot_rows(grad_scores, queries) * scale)
+        grad_query_ref[start:reach, :] = jnp.concatenate(query_grads, axis=1)
+        key_grads = jnp.concatenate(key_grads, axis=1)
+        value_grads = jnp.concatenate(value_grads, axis=1)
+        if reach == count_of_rows:
+            grad_key_ref[...] = key_grads
+            grad_value_ref[...] = value_grads
+        else:
+            grad_key_ref[:reach, :] += key_grads
+            grad_value_ref[:reach, :] += value_grads
+
+
+def row_spec(size, width):
+    return pl.BlockSpec((size, width), lambda index: (index, 0))
+
+
+def call_attention(kernel, segment, arrays, outputs):
+    size = segment.shape[0] // MICRO
+    return pl.pallas_call(
+        kernel,
+        grid=(MICRO,),
+        in_specs=[row_spec(size, 1), pl.BlockSpec((1, 1, size), lambda index: (index, 0, 0))]
+        + [row_spec(size, item.shape[1]) for item in arrays],
+        out_specs=[row_spec(size, item.shape[1]) for item in outputs],
+        out_shape=outputs,
+        compiler_params=pltpu.CompilerParams(vmem_limit_bytes=50 * 2**20),
+    )(segment.reshape(-1, 1), segment.reshape(MICRO, 1, size), *arrays)
+
+
+def attend(query_rows, key_rows, value_rows, segment):
     count_of_rows = query_rows.shape[0]
-    queries = query_rows.reshape(
-        count_of_rows, KEY_VALUE_HEADS, QUERY_HEADS // KEY_VALUE_HEADS, HEAD_WIDTH
-    )
-    keys = key_rows.reshape(count_of_rows, KEY_VALUE_HEADS, HEAD_WIDTH)
-    values = value_rows.reshape(count_of_rows, KEY_VALUE_HEADS, HEAD_WIDTH)
-    scores = jnp.einsum(
-        "qgjd,kgd->gjqk", queries, keys, preferred_element_type=jnp.float32
-    ) * HEAD_WIDTH ** (-0.5)
-    scores = jnp.where(allowed, scores, masked_fill)
-    peak = jnp.max(scores, axis=-1, keepdims=True)
-    expo = jnp.exp(scores - peak)
-    total = jnp.sum(expo, axis=-1, keepdims=True)
-    probs = (expo / total).astype(jnp.bfloat16)
-    mixed = jnp.einsum("gjqk,kgd->qgjd", probs, values, preferred_element_type=jnp.float32)
-    mixed = mixed.reshape(count_of_rows, QUERY_HEADS * HEAD_WIDTH).astype(jnp.bfloat16)
-    return (mixed, peak + jnp.log(total))
-
-
-def attention_backward(query_rows, key_rows, value_rows, log_total, mixed_gradient, allowed):
-    count_of_rows = query_rows.shape[0]
-    scale = HEAD_WIDTH ** (-0.5)
-    group_shape = (count_of_rows, KEY_VALUE_HEADS, QUERY_HEADS // KEY_VALUE_HEADS, HEAD_WIDTH)
-    queries = query_rows.reshape(group_shape)
-    keys = key_rows.reshape(count_of_rows, KEY_VALUE_HEADS, HEAD_WIDTH)
-    values = value_rows.reshape(count_of_rows, KEY_VALUE_HEADS, HEAD_WIDTH)
-    mixed_gradient = mixed_gradient.reshape(group_shape)
-    scores = jnp.einsum("qgjd,kgd->gjqk", queries, keys, preferred_element_type=jnp.float32) * scale
-    scores = jnp.where(allowed, scores, masked_fill)
-    probs_full = jnp.exp(scores - log_total)
-    probs = probs_full.astype(jnp.bfloat16)
-    value_gradient = jnp.einsum(
-        "gjqk,qgjd->kgd", probs, mixed_gradient, preferred_element_type=jnp.float32
-    )
-    grad_probs = jnp.einsum(
-        "qgjd,kgd->gjqk", mixed_gradient, values, preferred_element_type=jnp.float32
-    )
-    row_weight = jnp.sum(probs_full * grad_probs, axis=-1, keepdims=True)
-    grad_scores = (probs_full * (grad_probs - row_weight)).astype(jnp.bfloat16)
-    grad_queries = (
-        jnp.einsum("gjqk,kgd->qgjd", grad_scores, keys, preferred_element_type=jnp.float32) * scale
-    )
-    key_gradient = (
-        jnp.einsum("gjqk,qgjd->kgd", grad_scores, queries, preferred_element_type=jnp.float32)
-        * scale
-    )
-    return (
-        grad_queries.reshape(count_of_rows, -1),
-        key_gradient.reshape(count_of_rows, -1),
-        value_gradient.reshape(count_of_rows, -1),
+    return call_attention(
+        forward_kernel,
+        segment,
+        (query_rows, key_rows, value_rows),
+        [
+            jax.ShapeDtypeStruct(query_rows.shape, jnp.bfloat16),
+            jax.ShapeDtypeStruct((count_of_rows, QUERY_HEADS), jnp.float32),
+        ],
+    )
+
+
+def attend_back(query_rows, key_rows, value_rows, log_total, mixed_gradient, segment):
+    return call_attention(
+        backward_kernel,
+        segment,
+        (query_rows, key_rows, value_rows, log_total, mixed_gradient),
+        [
+            jax.ShapeDtypeStruct(item.shape, jnp.float32)
+            for item in (query_rows, key_rows, value_rows)
+        ],
     )
 
 
@@ -232,29 +331,6 @@
 def blocks_of(rows):
     size = rows.shape[0] // MICRO
     return [rows[index * size : (index + 1) * size] for index in range(MICRO)]
-
-
-def attend(query_rows, key_rows, value_rows, allowed):
-    results = [
-        attention_forward(*piece)
-        for piece in zip(blocks_of(query_rows), blocks_of(key_rows), blocks_of(value_rows), allowed)
-    ]
-    return (jnp.concatenate([item[0] for item in results]), [item[1] for item in results])
-
-
-def attend_back(query_rows, key_rows, value_rows, log_total, mixed_gradient, allowed):
-    results = [
-        attention_backward(*piece)
-        for piece in zip(
-            blocks_of(query_rows),
-            blocks_of(key_rows),
-            blocks_of(value_rows),
-            log_total,
-            blocks_of(mixed_gradient),
-            allowed,
-        )
-    ]
-    return tuple(jnp.concatenate([item[member] for item in results]) for member in range(3))
 
 
 def sum_shards(buffer, last):
@@ -290,7 +366,7 @@
     kv = key_weight.shape[2]
     down_rows = down_weight.shape[1]
     layouts = [geometry(piece) for piece in blocks_of(segment)]
-    layout = ([item[0] for item in layouts],) + tuple(
+    layout = (segment,) + tuple(
         jnp.concatenate([item[member] for item in layouts]) for member in range(1, 4)
     )
     active_rows = layout[1]

time: 828 us -> 711 us (0.86)
  matrix products: 318 us -> 184 us
  Pallas kernels: 0 us -> 115 us
  other arithmetic: 130 us -> 63 us
  waiting for transfers between devices: 190 us -> 156 us
    dot_general x24 -> x0, matrix products: 146 us -> none  [the longest x4 53.3 us: attention_backward(): jnp.einsum('qgjd,kgd->gjqk', mixed_gradient, values, preferred_element_ty...]
    pallas_call x0 -> x4, Pallas kernels: none -> 115 us  [call_attention(): pl.pallas_call(kernel, grid=(MICRO,), in_specs=[row_spec(size, 1), pl.Blo...]
    convert_element_type x4 -> x0, other arithmetic: 56.9 us -> none  [attention_backward(): grad_scores = (probs_full * (grad_probs - row_weight)).astype(jnp.bfloat16)]
    all_gather x4, waiting for transfers between devices: 76.7 us -> 37 us  [local(): whole = lax.all_gather(packed, 'fsdp', axis=0, tiled=False)]
    convert_element_type x0 -> x6, local copies, waits for them, and re-layouts: none -> 16.4 us  [the longest x4 8.51 us: rotate_flat(): rotation(shaped, cosine_table, sine_values).reshape(rows.shape)]
    pallas_call x0 -> x4, local copies, waits for them, and re-layouts: none -> 14.5 us  [call_attention(): pl.pallas_call(kernel, grid=(MICRO,), in_specs=[row_spec(size, 1), pl.Blo...]
    unnamed x216 -> x190, local copies, waits for them, and re-layouts: 23.7 us -> 10.3 us
    reduce_sum x4 -> x0, other arithmetic: 13.3 us -> none  [attention_forward(): total = jnp.sum(expo, axis=-1, keepdims=True)]
  transfers between devices with their start and end apart: 11 -> 11, of which waited for: 7 -> 6; matrix products, arithmetic and copies ran while one was open for 27% -> 29% of each run, Pallas kernels for 0% -> 7%
where the time goes in v2:
time: 711 us; the launch traced here: 702 us
  matrix products  184 us (26%)
  waiting for transfers between devices  156 us (22%)
  Pallas kernels  115 us (16%)
  local copies, waits for them, and re-layouts  101 us (14%)
  other arithmetic  63 us (9%)
  blocking collectives  59.2 us (8%)
  between operations  16.7 us (2%)
    reduce_scatter x4, waiting for transfers between devices, sum_shards(): shard = lax.psum_scatter(buffer, 'fsdp', scatter_dimension=0, tiled=False)  118 us
    pallas_call x4, Pallas kernels, call_attention(): pl.pallas_call(kernel, grid=(MICRO,), in_specs=[row_spec(size, 1), pl.Blo...  115 us
    dot_general x14, matrix products, times_transposed(): lax.dot_general(left, right, (((1,), (1,)), ((), ())), preferred_element_...  58.4 us
    dot_general x14, matrix products, contract_rows(): lax.dot_general(left, right, (((0,), (0,)), ((), ())), preferred_element_...  57.8 us
    all_gather x4, waiting for transfers between devices, local(): whole = lax.all_gather(packed, 'fsdp', axis=0, tiled=False)  37 us
    all_gather x3, blocking collectives, sum_shards(): return lax.all_gather(part, 'rep', axis=0, tiled=True)  29.8 us
    unnamed x1, blocking collectives  29.4 us
    dot_general x2, matrix products, layer_forward(): jnp.dot(normed_feed, up_weight, preferred_element_type=jnp.float32)  21 us
  transfers between devices with their start and end apart: 11, of which 6 were waited for; matrix products, arithmetic and copies ran while one was open for 29% of the time, Pallas kernels for 7%

profile of v2, /device:TPU:0, one launch (start us, length us, event | category | flops | bytes accessed | tf_op | source)
XLA Modules:
  0.0 701.8 jit_solution(5025352950604371224)
XLA Ops:
  22.1 20.2 %all-gather.19.cloned.1.call-done = bf16[8,73,1536]{2,1,0:T(8,128)(2,1)} async-done(((bf16[1,73,1536]{2,1,0:T(8,128)(2,1)}), bf16[8,73,1536]{2,1,0:T(8,128)(2,1)}) %all-gather.19.cloned.1.call-update) | async-done | bytes 1794064 | tf_op jit(solution)/shard_map/all_gather | solution.py:384
  59.5 24.5 %shard_map.203 = (bf16[1536,576]{1,0:T(8,128)(2,1)}, f32[1536,9]{1,0:T(8,128)S(1)}) custom-call(s32[1536,1]{1,0:T(8,128)S(1)} %reshape.454.column_ref, s32[2,1,768]{2,1,0:T(1,128)S(1)} %reshape.403.row_ref, bf16[1536,576]{1,0:T(8,128)(2,1)} %copy.125.query_ref, bf16[1536,192]{1,0:T(8,128)(2,1)S(1)} %copy.126.key_ref, ...), custom_call_target="tpu_custom_call" | custom-call | tf_op jit(solution)/shard_map/pallas_call | solution.py:187
  84.0 5.8 multiply_reduce_fusion.8
  109.4 6.0 fusion.82
  115.5 7.9 %multiply_convert_fusion.1 = (bf16[1536,1536]{1,0:T(8,128)(2,1)S(1)}, f32[1536,1536]{1,0:T(8,128)}) fusion(f32[1536,1536]{1,0:T(8,128)S(1)} %fusion.82, bf16[1536,576]{0,1:T(8,128)(2,1)S(1)} %copy-done.37, bf16[576,1536]{1,0:T(8,128)(2,1)S(1)} %bitcast.185), kind=kOutput, calls=%fused_computation.15 | convolution fusion | flops 2732064768 | bytes 27131904 | tf_op jit(solution)/shard_map/dot_general | solution.py:248
  143.9 24.0 %shard_map.204 = (bf16[1536,576]{1,0:T(8,128)(2,1)}, f32[1536,9]{1,0:T(8,128)S(1)}) custom-call(s32[1536,1]{1,0:T(8,128)S(1)} %reshape.454.column_ref, s32[2,1,768]{2,1,0:T(1,128)S(1)} %reshape.403.row_ref, bf16[1536,576]{1,0:T(8,128)(2,1)} %copy.129.query_ref, bf16[1536,192]{1,0:T(8,128)(2,1)S(1)} %copy.130.key_ref, ...), custom_call_target="tpu_custom_call" | custom-call | tf_op jit(solution)/shard_map/pallas_call | solution.py:187
  167.9 5.7 multiply_reduce_fusion.6
  174.2 11.5 %all-gather.17.cloned.1.call-done = bf16[1728,1536]{1,0:T(8,128)(2,1)} async-done(((bf16[216,1536]{1,0:T(8,128)(2,1)}), bf16[1728,1536]{1,0:T(8,128)(2,1)}) %all-gather.17.cloned.1.call-update) | async-done | bytes 5308432 | tf_op jit(solution)/shard_map/all_gather | solution.py:400
  190.8 5.7 reshape.416
  199.0 6.4 fusion.83
  205.4 5.7 convolution_convert_fusion.1
  211.1 13.1 %fusion.4 = (bf16[1536,1536]{1,0:T(8,128)(2,1)}, bf16[1536,1536]{1,0:T(8,128)(2,1)}, bf16[1536,1536]{1,0:T(8,128)(2,1)S(1)}) fusion(bf16[1536,1536]{1,0:T(8,128)(2,1)} %convolution_convert_fusion.1, f32[1536,1536]{1,0:T(8,128)} %fusion.83, bf16[1536,576]{0,1:T(8,128)(2,1)S(1)} %multiply_convert_fusion.5, bf16[576,1536]{1,0:T(8,128)(2,1)S(1)} %bitcast.191), kind=kOutput, calls=%fused_computation.6 | convolution fusion | flops 2755657728 | bytes 31850496 | tf_op jit(solution)/shard_map/dot_general | solution.py:248
  224.2 6.6 fusion.84
  247.0 33.3 %shard_map.205 = (f32[1536,576]{1,0:T(8,128)}, f32[1536,192]{1,0:T(8,128)}, f32[1536,192]{1,0:T(8,128)}) custom-call(s32[1536,1]{1,0:T(8,128)S(1)} %reshape.454.column_ref, s32[2,1,768]{2,1,0:T(1,128)S(1)} %reshape.403.row_ref, bf16[1536,576]{1,0:T(8,128)(2,1)} %copy.129.query_ref, bf16[1536,192]{1,0:T(8,128)(2,1)S(1)} %copy.130.key_ref, ...), custom_call_target="tpu_custom_call" | custom-call | tf_op jit(solution)/shard_map/pallas_call | solution.py:187
  303.8 14.9 %fusion.9 = (bf16[1536,1536]{1,0:T(8,128)(2,1)}, bf16[1536,1536]{1,0:T(8,128)(2,1)}) fusion(f32[1536,1536]{1,0:T(8,128)} %copy-done.89, f32[1536,1536]{1,0:T(8,128)} %get-tuple-element.131, bf16[1536,576]{1,0:T(8,128)(2,1)S(1)} %copy-done.35, f32[1536,576]{0,1:T(8,128)S(1)} %subtract_add_fusion.1, f32[1536]{0:T(1024)S(1)} %copy-done.79), kind=kOutput, calls=%fused_computation.11 | convolution fusion | flops 2755067904 | bytes 33626112 | tf_op jit(solution)/shard_map/dot_general | solution.py:280
  318.7 5.5 fusion.85
  340.0 33.3 %shard_map.206 = (f32[1536,576]{1,0:T(8,128)}, f32[1536,192]{1,0:T(8,128)}, f32[1536,192]{1,0:T(8,128)}) custom-call(s32[1536,1]{1,0:T(8,128)S(1)} %reshape.454.column_ref, s32[2,1,768]{2,1,0:T(1,128)S(1)} %reshape.403.row_ref, bf16[1536,576]{1,0:T(8,128)(2,1)} %copy.125.query_ref, bf16[1536,192]{1,0:T(8,128)(2,1)S(1)} %copy.126.key_ref, ...), custom_call_target="tpu_custom_call" | custom-call | tf_op jit(solution)/shard_map/pallas_call | solution.py:187
  389.0 5.4 copy.141
  419.4 6.4 convolution_convert_fusion.3
  432.3 7.2 %convolution_convert_fusion.9 = bf16[576,1536]{1,0:T(8,128)(2,1)} fusion(bf16[1536,576]{0,1:T(8,128)(2,1)} %multiply_convert_fusion.7, bf16[1536,1536]{1,0:T(8,128)(2,1)} %get-tuple-element.52), kind=kOutput, calls=%fused_computation.71 | convolution fusion | flops 2718793728 | bytes 8257536 | tf_op jit(solution)/shard_map/dot_general | solution.py:274
  439.5 6.4 convolution_convert_fusion.8
  447.5 10.3 %reduce-scatter.9.cloned.1.call-done = bf16[1,73,1536]{2,1,0:T(8,128)(2,1)} async-done(((bf16[8,73,1536]{2,1,0:T(8,128)(2,1)}), bf16[1,73,1536]{2,1,0:T(8,128)(2,1)}) %reduce-scatter.9.cloned.1.call-update) | async-done | bytes 224272 | tf_op jit(solution)/shard_map/reduce_scatter | solution.py:337
  463.0 5.9 convolution_convert_fusion.2
  475.7 5.9 convolution_convert_fusion.7
  492.3 6.1 fusion.18
  498.5 6.7 add_convert_fusion
  506.0 9.3 %all-gather.5 = bf16[4,19,1536]{2,1,0:T(8,128)(2,1)S(1)} all-gather(bf16[1,19,1536]{2,1,0:T(8,128)(2,1)S(1)} %dynamic-slice_bitcast_fusion.2), channel_id=1, replica_groups=mesh['rep'=4,'fsdp'=8] {'rep'}, dimensions={0}, use_global_device_ids=true | all-gather | bytes 291840 | tf_op jit(solution)/shard_map/all_gather | solution.py:346
  521.2 46.8 %reduce-scatter.13.cloned.1.call-done = bf16[1,216,1536]{2,1,0:T(8,128)(2,1)} async-done(((bf16[8,216,1536]{2,1,0:T(8,128)(2,1)}), bf16[1,216,1536]{2,1,0:T(8,128)(2,1)}) %reduce-scatter.13.cloned.1.call-update) | async-done | bytes 663568 | tf_op jit(solution)/shard_map/reduce_scatter | solution.py:337
  568.0 61.4 %reduce-scatter.15.cloned.1.call-done = bf16[1,216,1536]{2,1,0:T(8,128)(2,1)} async-done(((bf16[8,216,1536]{2,1,0:T(8,128)(2,1)}), bf16[1,216,1536]{2,1,0:T(8,128)(2,1)}) %reduce-scatter.15.cloned.1.call-update) | async-done | bytes 663568 | tf_op jit(solution)/shard_map/reduce_scatter | solution.py:337
  629.3 29.4 %fusion.72 = (bf16[64,1536]{1,0:T(8,128)(2,1)S(1)}, bf16[64,1536]{1,0:T(8,128)(2,1)S(1)}) fusion(bf16[216,1536]{1,0:T(8,128)(2,1)} %bitcast.199, bf16[216,1536]{1,0:T(8,128)(2,1)} %bitcast.198), kind=kCustom, calls=%all-reduce-scatter.2 | all-reduce-scatter fusion | flops 786433 | bytes 1720832
  666.7 11.0 %all-gather.6 = bf16[4,54,1536]{2,1,0:T(8,128)(2,1)S(1)} all-gather(bf16[1,54,1536]{2,1,0:T(8,128)(2,1)S(1)} %dynamic-slice_bitcast_fusion.1), channel_id=1, replica_groups=mesh['rep'=4,'fsdp'=8] {'rep'}, dimensions={0}, use_global_device_ids=true | all-gather | bytes 829440 | tf_op jit(solution)/shard_map/all_gather | solution.py:346
  679.1 9.5 %all-gather.7 = bf16[4,54,1536]{2,1,0:T(8,128)(2,1)S(1)} all-gather(bf16[1,54,1536]{2,1,0:T(8,128)(2,1)S(1)} %dynamic-slice_bitcast_fusion), channel_id=1, replica_groups=mesh['rep'=4,'fsdp'=8] {'rep'}, dimensions={0}, use_global_device_ids=true | all-gather | bytes 829440 | tf_op jit(solution)/shard_map/all_gather | solution.py:346
  (366 shorter events, 227.6 us)
Async XLA Ops:
  7.2 35.1 %all-gather.19.cloned.1.call-start = ((), (), s32[]{:S(2)}) async-start(), calls=%async_computation.11 | async-start | bytes 2211840 | tf_op jit(solution)/shard_map/all_gather | solution.py:384
  11.5 89.2 %all-gather.13.cloned.1.call-start = ((), (), s32[]{:S(2)}) async-start(), calls=%async_computation.8 | async-start | bytes 5971968 | tf_op jit(solution)/shard_map/all_gather | solution.py:400
  15.2 114.2 %all-gather.15.cloned.1.call-start = ((), (), s32[]{:S(2)}) async-start(), calls=%async_computation.9 | async-start | bytes 1990656 | tf_op jit(solution)/shard_map/all_gather | solution.py:384
  17.0 168.8 %all-gather.17.cloned.1.call-start = ((), (), s32[]{:S(2)}) async-start(), calls=%async_computation.10 | async-start | bytes 5971968 | tf_op jit(solution)/shard_map/all_gather | solution.py:400
  18.3 427.6 %reduce-scatter.11.cloned.1.call-start = ((), (), s32[]{:S(2)}) async-start(), calls=%async_computation.5 | async-start | bytes 2211840 | tf_op jit(solution)/shard_map/reduce_scatter | solution.py:337
  19.7 30.0 %copy-start.62 = (f32[1536]{0:T(1024)}, f32[1536]{0:T(1024)S(1)}, u32[]{:S(2)}) copy-start(f32[1536]{0:T(1024)S(1)} %get-tuple-element.109) | copy-start | bytes 18436
  22.1 29.2 %copy-start.13 = (f32[1536,32]{0,1:T(8,128)}, f32[1536,32]{0,1:T(8,128)S(1)}, u32[]{:S(2)}) copy-start(f32[1536,32]{0,1:T(8,128)S(1)} %maximum_bitcast_fusion.1) | copy-start | bytes 589828
  22.1 101.5 %copy-start.76 = (f32[1536]{0:T(1024)}, f32[1536]{0:T(1024)S(1)}, u32[]{:S(2)}) copy-start(f32[1536]{0:T(1024)S(1)} %maximum_reduce_fusion) | copy-start | bytes 18436
  50.8 8.7 %copy-start = (bf16[1536,192]{1,0:T(8,128)(2,1)}, bf16[1536,192]{1,0:T(8,128)(2,1)S(1)}, u32[]{:S(2)}) copy-start(bf16[1536,192]{1,0:T(8,128)(2,1)S(1)} %convolution_convert_fusion.11.value_ref) | copy-start | bytes 1769476
  59.5 24.5 %copy-start.18 = (bf16[1536,576]{0,1:T(8,128)(2,1)S(1)}, bf16[1536,576]{0,1:T(8,128)(2,1)}, u32[]{:S(2)}) copy-start(bf16[1536,576]{0,1:T(8,128)(2,1)} %param.12) | copy-start | bytes 5308420
  89.9 10.8 %copy-start.70 = (f32[576]{0:T(1024)}, f32[576]{0:T(1024)S(1)}, u32[]{:S(2)}) copy-start(f32[576]{0:T(1024)S(1)} %mul.691) | copy-start | bytes 6916
  91.8 8.9 %copy-start.59 = (f32[1536]{0:T(1024)}, f32[1536]{0:T(1024)S(1)}, u32[]{:S(2)}) copy-start(f32[1536]{0:T(1024)S(1)} %get-tuple-element.111) | copy-start | bytes 18436
  115.4 8.2 %copy-start.89 = (f32[1536,1536]{1,0:T(8,128)}, f32[1536,1536]{1,0:T(8,128)S(1)}, u32[]{:S(2)}) copy-start(f32[1536,1536]{1,0:T(8,128)S(1)} %fusion.82) | copy-start | bytes 28311556
  115.5 8.2 %copy-start.23 = (f32[1536,576]{0,1:T(8,128)S(1)}, f32[1536,576]{0,1:T(8,128)}, u32[]{:S(2)}) copy-start(f32[1536,576]{0,1:T(8,128)} %get-tuple-element.129) | copy-start | bytes 10616836
  115.5 8.2 %copy-start.34 = (bf16[1536,576]{1,0:T(8,128)(2,1)S(1)}, bf16[1536,576]{1,0:T(8,128)(2,1)}, u32[]{:S(2)}) copy-start(bf16[1536,576]{1,0:T(8,128)(2,1)} %reshape.410) | copy-start | bytes 5308420
  141.4 26.5 %copy-start.7 = (f32[1536,576]{0,1:T(8,128)S(1)}, f32[1536,576]{0,1:T(8,128)}, u32[]{:S(2)}) copy-start(f32[1536,576]{0,1:T(8,128)} %copy-done.6) | copy-start | bytes 10616836
  141.4 26.5 %copy-start.77 = (f32[1536]{0:T(1024)S(1)}, f32[1536]{0:T(1024)}, u32[]{:S(2)}) copy-start(f32[1536]{0:T(1024)} %copy-done.76) | copy-start | bytes 18436
  199.0 12.2 %copy-start.39 = (bf16[1536,576]{0,1:T(8,128)(2,1)}, bf16[1536,576]{0,1:T(8,128)(2,1)S(1)}, u32[]{:S(2)}) copy-start(bf16[1536,576]{0,1:T(8,128)(2,1)S(1)} %multiply_convert_fusion.5) | copy-start | bytes 5308420
  224.2 6.6 copy-start.87
  224.2 6.6 copy-start.9
  224.2 6.6 copy-start.61
  224.2 6.6 copy-start.69
  303.1 25.5 %copy-start.20 = (f32[1536,576]{0,1:T(8,128)}, f32[1536,576]{0,1:T(8,128)S(1)}, u32[]{:S(2)}) copy-start(f32[1536,576]{0,1:T(8,128)S(1)} %subtract_add_fusion.1) | copy-start | bytes 10616836
  387.1 70.7 %reduce-scatter.9.cloned.1.call-start = ((), (), s32[]{:S(2)}) async-start(), calls=%async_computation.4 | async-start | bytes 2211840 | tf_op jit(solution)/shard_map/reduce_scatter | solution.py:337
  387.2 7.2 %copy-start.29 = (bf16[1536,3,64]{0,2,1:T(8,128)(2,1)}, bf16[1536,3,64]{0,2,1:T(8,128)(2,1)S(1)}, u32[]{:S(2)}) copy-start(bf16[1536,3,64]{0,2,1:T(8,128)(2,1)S(1)} %pad_maximum_fusion.16) | copy-start | bytes 1769476
  419.4 85.8 %all-reduce.13.cloned.1.call-start = ((), (), s32[]{:S(2)}) async-start(), calls=%async_computation.12 | async-start | bytes 983040
  432.3 7.2 %copy-start.38 = (bf16[1536,576]{0,1:T(8,128)(2,1)S(1)}, bf16[1536,576]{0,1:T(8,128)(2,1)}, u32[]{:S(2)}) copy-start(bf16[1536,576]{0,1:T(8,128)(2,1)} %multiply_convert_fusion.7) | copy-start | bytes 5308420
  457.9 110.1 %reduce-scatter.13.cloned.1.call-start = ((), (), s32[]{:S(2)}) async-start(), calls=%async_computation.6 | async-start | bytes 5971968 | tf_op jit(solution)/shard_map/reduce_scatter | solution.py:337
  463.0 166.3 %reduce-scatter.15.cloned.1.call-start = ((), (), s32[]{:S(2)}) async-start(), calls=%async_computation.7 | async-start | bytes 5971968 | tf_op jit(solution)/shard_map/reduce_scatter | solution.py:337
  658.7 8.0 %copy-start.49 = (bf16[64,1536]{1,0:T(8,128)(2,1)}, bf16[64,1536]{1,0:T(8,128)(2,1)S(1)}, u32[]{:S(2)}) copy-start(bf16[64,1536]{1,0:T(8,128)(2,1)S(1)} %get-tuple-element.47) | copy-start | bytes 589828
  658.8 7.6 %collective-permute-start = (bf16[30,1536]{1,0:T(8,128)(2,1)S(1)}, bf16[30,1536]{1,0:T(8,128)(2,1)S(1)}, u32[]{:S(2)}, u32[]{:S(2)}) collective-permute-start(bf16[30,1536]{1,0:T(8,128)(2,1)S(1)} %slice.352), channel_id=1, source_target_pairs={{0,8},{8,16},{16,24},{1,9},{9,17},{17,25},{2,10},{10,18},{18,26},{... | collective-permute-start | bytes 276488
  663.1 15.2 %collective-permute-start.1 = (bf16[30,1536]{1,0:T(8,128)(2,1)}, bf16[30,1536]{1,0:T(8,128)(2,1)S(1)}, u32[]{:S(2)}, u32[]{:S(2)}) collective-permute-start(bf16[30,1536]{1,0:T(8,128)(2,1)} %slice.353), channel_id=1, source_target_pairs={{0,8},{8,16},{16,24},{1,9},{9,17},{17,25},{2,10},{10,18},{18,26},{... | collective-permute-start | bytes 276488
  (70 other events, 259.4 us)
Sparse Core Ops, SparseCore 0:
  11.6 30.7 all-gather.18
  44.5 56.0 all-gather.12
  102.9 25.1 all-gather.14
  129.6 56.1 all-gather.16
  387.2 34.2 reduce-scatter.10
  423.8 33.9 reduce-scatter.8
  461.4 43.5 all-reduce.12
  507.4 60.5 reduce-scatter.12
  570.4 58.8 reduce-scatter.14
